TPU v7x, 128 devices: a whole 4x4x4 slice. The times are simulated.
128 devices in a mesh: row: 16 (over z, y_lo, core), col: 8 (over x, y_hi).
Axes of the slice: x: 4, y: 4 (y_hi: 2, y_lo: 2; y = y_hi * 2 + y_lo), z: 4, core: 2. Of those that a mesh axis runs over, the one named last changes fastest.
Arguments:
- pair: bfloat16 [512, 512, 128], P('row', 'col'), may hold values from -6 to 6
- residue_mask: int32 [512], replicated, may hold values 0 or 1
- out_in_w: bfloat16 [128, 512], replicated, may hold values from -0.5 to 0.5
- out_gate_w: bfloat16 [128, 128], replicated, may hold values from -0.5 to 0.5
- out_out_w: bfloat16 [128, 128], replicated, may hold values from -0.5 to 0.5
- inc_in_w: bfloat16 [128, 512], replicated, may hold values from -0.5 to 0.5
- inc_gate_w: bfloat16 [128, 128], replicated, may hold values from -0.5 to 0.5
- inc_out_w: bfloat16 [128, 128], replicated, may hold values from -0.5 to 0.5
- trans_up: bfloat16 [128, 1024], replicated, may hold values from -0.5 to 0.5
- trans_down: bfloat16 [512, 128], replicated, may hold values from -0.25 to 0.25
Outputs:
- updated: bfloat16 [512, 512, 128], P('row', 'col')
All inputs are finite; a program needn't handle non-finite values.
Results may differ from a plain program's by a relative error of at most 0.014.
Values may be sent and summed in bfloat16 or wider, within the bound.
No kernel may reach another device: no remote copies, remote signals or barrier semaphores. Data moves between devices by JAX's collectives and lax.ppermute only.
A program may use at most 128 MiB of HBM per device.

v0:
```python
import jax
import jax.numpy as jnp
from jax import lax
from jax.sharding import PartitionSpec as P


def from_root(block, axis, holder):
    block = jnp.where(lax.axis_index(axis) == holder, block, jnp.zeros_like(block))
    return lax.psum(block, axis)


def layer_norm(values):
    center = values - jnp.mean(values, axis=-1, keepdims=True)
    spread = jnp.mean(center * center, axis=-1, keepdims=True)
    return center * lax.rsqrt(spread + 1e-05)


def project_tile(pair, tile_mask, w_in, w_gate):
    rows, cols, chans = pair.shape
    width = w_in.shape[1] // 4
    pair_f = pair.astype(jnp.float32)
    flat = layer_norm(pair_f).astype(jnp.bfloat16).reshape(rows * cols, chans)
    projected = jnp.dot(flat, w_in, preferred_element_type=jnp.float32).reshape(
        rows, cols, 4 * width
    )
    masked = tile_mask[:, :, None]
    left = (
        masked * jax.nn.sigmoid(projected[..., 0:width]) * projected[..., width : 2 * width]
    ).astype(jnp.bfloat16)
    right = (
        masked
        * jax.nn.sigmoid(projected[..., 2 * width : 3 * width])
        * projected[..., 3 * width : 4 * width]
    ).astype(jnp.bfloat16)
    gate = jax.nn.sigmoid(jnp.dot(flat, w_gate, preferred_element_type=jnp.float32)).reshape(
        rows, cols, chans
    )
    return (pair_f, jnp.transpose(left, (2, 0, 1)), jnp.transpose(right, (2, 0, 1)), gate)


def finish_tile(pair_f, mixed, gate, w_out):
    centered = mixed - jnp.mean(mixed, axis=0, keepdims=True)
    spread = jnp.mean(centered * centered, axis=0, keepdims=True)
    scaled = (centered * lax.rsqrt(jnp.maximum(spread, 1.0))).astype(jnp.bfloat16)
    update = jnp.einsum("hij,hc->ijc", scaled, w_out, preferred_element_type=jnp.float32)
    return (pair_f + gate * update).astype(jnp.bfloat16)


def on_device(
    pair,
    residue_mask,
    out_in_w,
    out_gate_w,
    out_out_w,
    inc_in_w,
    inc_gate_w,
    inc_out_w,
    trans_up,
    trans_down,
):
    row_idx = lax.axis_index("row")
    col_idx = lax.axis_index("col")
    rows, cols, chans = pair.shape
    present = residue_mask.astype(jnp.float32)
    row_mask = lax.dynamic_slice_in_dim(present, row_idx * rows, rows)
    col_mask = lax.dynamic_slice_in_dim(present, col_idx * cols, cols)
    tile_mask = row_mask[:, None] * col_mask[None, :]
    pair_f, left, right, gate = project_tile(pair, tile_mask, out_in_w, out_gate_w)
    right_rows = lax.all_gather(right, "col", axis=2, tiled=True)
    partner = jnp.concatenate(
        [from_root(right_rows, "row", 2 * col_idx + which) for which in range(2)], axis=1
    )
    mixed = jnp.einsum(
        "hik,hjk->hij",
        lax.all_gather(left, "col", axis=2, tiled=True),
        partner,
        preferred_element_type=jnp.float32,
    )
    first = finish_tile(pair_f, mixed, gate, out_out_w)
    first_f, left, right, gate = project_tile(first, tile_mask, inc_in_w, inc_gate_w)
    left_all, right_all = (
        lax.all_gather(left, "row", axis=1, tiled=True),
        lax.all_gather(right, "row", axis=1, tiled=True),
    )
    offset = row_idx % 2 * rows
    owner = row_idx // 2
    received = from_root(left_all, "col", owner)
    left_cols = lax.dynamic_slice_in_dim(received, offset, rows, 2)
    mixed = jnp.einsum("hki,hkj->hij", left_cols, right_all, preferred_element_type=jnp.float32)
    second = finish_tile(first_f, mixed, gate, inc_out_w)
    second_f = second.astype(jnp.float32)
    normed = layer_norm(second_f).astype(jnp.bfloat16).reshape(rows * cols, chans)
    raised = jnp.dot(normed, trans_up, preferred_element_type=jnp.float32)
    inner = trans_down.shape[0]
    hidden = (jax.nn.silu(raised[:, 0:inner]) * raised[:, inner : 2 * inner]).astype(jnp.bfloat16)
    lowered = jnp.dot(hidden, trans_down, preferred_element_type=jnp.float32).reshape(
        rows, cols, chans
    )
    return (second_f + lowered).astype(jnp.bfloat16)


def solution(mesh):
    in_specs = (P("row", "col", None), P(), P(), P(), P(), P(), P(), P(), P(), P())
    out_specs = P("row", "col", None)
    return jax.shard_map(
        on_device, mesh=mesh, in_specs=in_specs, out_specs=out_specs, check_vma=False
    )
```

profile of v0, /device:TPU:1, one launch (start us, length us, event | category | flops | bytes accessed | tf_op | source)
XLA Modules:
  0.0 864.7 jit_solution(1791962962403467293)
XLA Ops:
  6.5 0.7 convert_element_type.53
  7.4 1.4 convert_reduce_fusion.2
  8.8 1.7 fusion.23
  10.5 1.6 fusion.24
  12.3 1.6 fusion.54
  13.8 1.6 fusion.49
  15.5 0.7 all-gather.5.cloned.1.call-update
  16.3 73.6 %all-gather.7.cloned.1.call-done = bf16[128,32,512]{0,2,1:T(8,128)(2,1)} async-done(((bf16[128,32,64]{0,2,1:T(8,128)(2,1)}), bf16[128,32,512]{0,2,1:T(8,128)(2,1)}) %all-gather.7.cloned.1.call-update) | async-done | bytes 4194320 | tf_op jit(solution)/shard_map/all_gather | solution.py:69
  89.9 6.0 broadcast_select_fusion.2
  96.0 0.7 copy-done.6
  97.1 64.5 %all-gather.5.cloned.1.call-done = bf16[128,32,512]{0,2,1:T(8,128)(2,1)} async-done(((bf16[128,32,64]{0,2,1:T(8,128)(2,1)}), bf16[128,32,512]{0,2,1:T(8,128)(2,1)}) %all-gather.5.cloned.1.call-update) | async-done | bytes 4194320 | tf_op jit(solution)/shard_map/all_gather | solution.py:75
  161.6 7.9 copy.17
  169.6 187.0 %all-reduce.6.cloned.1.call-done = (bf16[128,32,512]{0,2,1:T(8,128)(2,1)}, bf16[128,32,512]{0,2,1:T(8,128)(2,1)}) async-done(((bf16[128,32,512]{0,2,1:T(8,128)(2,1)}, bf16[128,32,512]{0,2,1:T(8,128)(2,1)}), (bf16[128,32,512]{0,2,1:T(8,128)(2,1)}, bf16[128,32,512]{0,2,1:T(8,128)(2,1)})) %all-reduce.6.cloned.1.call-update) | async-done | bytes 8388624 | tf_op jit(solution)/shard_map/psum | solution.py:9
  356.6 7.4 pad_maximum_fusion
  364.0 12.5 %copy.18 = bf16[128,64,512]{2,1,0:T(8,128)(2,1)} copy(bf16[128,64,512]{0,2,1:T(8,128)(2,1)} %pad_maximum_fusion) | data formatting | bytes 16777216 | tf_op jit(solution)/shard_map/concatenate | solution.py:70
  376.6 7.0 fusion.60
  384.6 0.8 convert_reduce_fusion.1
  386.6 0.7 fusion.52
  387.3 1.6 fusion.50
  389.8 52.2 %all-gather.9.cloned.1.call-done = bf16[128,512,64]{0,2,1:T(8,128)(2,1)} async-done(((bf16[128,32,64]{0,2,1:T(8,128)(2,1)}), bf16[128,512,64]{0,2,1:T(8,128)(2,1)}) %all-gather.9.cloned.1.call-update) | async-done | bytes 8388624 | tf_op jit(solution)/shard_map/all_gather | solution.py:82
  442.1 13.6 %copy.20 = bf16[128,512,64]{1,2,0:T(8,128)(2,1)} copy(bf16[128,512,64]{0,2,1:T(8,128)(2,1)} %all-gather.9.cloned.1.call-done) | data formatting | bytes 16777216 | tf_op jit(solution)/shard_map/all_gather | solution.py:82
  455.7 7.2 broadcast_select_fusion
  462.9 0.7 copy-done.7
  464.1 32.7 %all-gather.11.cloned.1.call-done = bf16[128,512,64]{0,2,1:T(8,128)(2,1)} async-done(((bf16[128,32,64]{0,2,1:T(8,128)(2,1)}), bf16[128,512,64]{0,2,1:T(8,128)(2,1)}) %all-gather.11.cloned.1.call-update) | async-done | bytes 8388624 | tf_op jit(solution)/shard_map/all_gather | solution.py:83
  496.8 23.8 %copy.21 = bf16[128,512,64]{2,1,0:T(8,128)(2,1)} copy(bf16[128,512,64]{0,2,1:T(8,128)(2,1)} %all-gather.11.cloned.1.call-done) | data formatting | bytes 16777216 | tf_op jit(solution)/shard_map/all_gather | solution.py:83
  520.5 321.2 %all-reduce.4.cloned.1.call-done = bf16[128,512,64]{1,2,0:T(8,128)(2,1)} async-done(((bf16[128,512,64]{1,2,0:T(8,128)(2,1)}), bf16[128,512,64]{1,2,0:T(8,128)(2,1)}) %all-reduce.4.cloned.1.call-update) | async-done | bytes 8388624 | tf_op jit(solution)/shard_map/psum | solution.py:9
  841.7 9.7 %fusion.61 = (f32[32,64]{1,0:T(8,128)S(1)}, f32[128,32,64]{2,1,0:T(8,128)S(1)}) fusion(bf16[128,512,64]{2,1,0:T(8,128)(2,1)} %copy.21, bf16[128,512,64]{1,2,0:T(8,128)(2,1)} %all-reduce.4.cloned.1.call-done, s32[]{:T(128)S(6)} %select_n.52), kind=kOutput, calls=%fused_computation.101 | convolution fusion | flops 268695552 | bytes 22028292 | tf_op jit(solution)/shard_map/hki,hkj->hij/dot_general | solution.py:89
  852.1 0.8 convert_reduce_fusion
  852.9 0.6 fusion.19
  854.2 1.2 fusion.62
  855.5 1.4 fusion.9
  856.9 0.9 fusion.25
  (47 shorter events, 5.7 us)
Async XLA Ops:
  6.5 847.7 %copy-start = (bf16[128,1024]{1,0:T(8,128)(2,1)S(1)}, bf16[128,1024]{1,0:T(8,128)(2,1)}, u32[]{:S(2)}) copy-start(bf16[128,1024]{1,0:T(8,128)(2,1)} %param.18) | copy-start | bytes 786436
  6.5 83.3 %all-gather.7.cloned.1.call-start = ((), (), s32[]{:S(2)}) async-start(), calls=%async_computation.1 | async-start | bytes 4718592 | tf_op jit(solution)/shard_map/all_gather | solution.py:69
  15.4 146.2 %all-gather.5.cloned.1.call-start = ((), (), s32[]{:S(2)}) async-start(), calls=%async_computation | async-start | bytes 4718592 | tf_op jit(solution)/shard_map/all_gather | solution.py:75
  16.2 340.4 %all-reduce.6.cloned.1.call-start = ((), (), s32[]{:S(2)}) async-start(), calls=%async_computation.5 | async-start | bytes 16777216 | tf_op jit(solution)/shard_map/psum | solution.py:9
  95.9 0.8 copy-start.6
  95.9 346.1 %all-gather.9.cloned.1.call-start = ((), (), s32[]{:S(2)}) async-start(), calls=%async_computation.2 | async-start | bytes 8912896 | tf_op jit(solution)/shard_map/all_gather | solution.py:82
  383.5 1.1 copy-start.1
  383.5 1.0 copy-start.3
  383.9 2.7 copy-start.2
  389.0 107.8 %all-gather.11.cloned.1.call-start = ((), (), s32[]{:S(2)}) async-start(), calls=%async_computation.4 | async-start | bytes 8912896 | tf_op jit(solution)/shard_map/all_gather | solution.py:83
  389.6 452.1 %all-reduce.4.cloned.1.call-start = ((), (), s32[]{:S(2)}) async-start(), calls=%async_computation.3 | async-start | bytes 16777216 | tf_op jit(solution)/shard_map/psum | solution.py:9
  462.9 0.8 copy-start.7
  851.4 0.8 copy-start.4
  854.2 1.3 copy-start.5
Sparse Core Ops, SparseCore 0:
  15.6 74.2 all-gather.6
  92.2 69.3 all-gather.4
  164.2 192.3 all-reduce.5
  389.1 52.9 all-gather.8
  443.6 53.1 all-gather.10
  499.1 342.5 all-reduce.3
where the time goes:
time: 872 us; the launch traced here: 865 us
  waiting for transfers between devices  733 us (84%)
  local copies, waits for them, and re-layouts  60 us (7%)
  other arithmetic  34.1 us (4%)
  matrix products  23.9 us (3%)
  between operations  13.8 us (2%)
    psum x2, waiting for transfers between devices, from_root(): return lax.psum(block, axis)  508 us
    all_gather x1, waiting for transfers between devices, on_device(): right_rows = lax.all_gather(right, 'col', axis=2, tiled=True)  73.6 us
    all_gather x1, waiting for transfers between devices, on_device(): lax.all_gather(left, 'col', axis=2, tiled=True)  64.5 us
    all_gather x1, waiting for transfers between devices, on_device(): lax.all_gather(left, 'row', axis=1, tiled=True)  52.2 us
    all_gather x1, waiting for transfers between devices, on_device(): lax.all_gather(right, 'row', axis=1, tiled=True)  32.7 us
    all_gather x1, local copies, waits for them, and re-layouts, on_device(): lax.all_gather(right, 'row', axis=1, tiled=True)  23.8 us
  transfers between devices with their start and end apart: 6, of which 6 were waited for; matrix products, arithmetic and copies ran while one was open for 7% of the time, Pallas kernels for 0%

commit v1 on v0

v1 whole, which is shorter than its diff:
```python
import functools

import jax
import jax.numpy as jnp
from jax import lax
from jax.experimental import pallas as pl
from jax.experimental.pallas import tpu as pltpu
from jax.sharding import PartitionSpec as P

F32 = jnp.float32
BF16 = jnp.bfloat16
ROWS, COLS, CHANS = 32, 64, 128
HALF = ROWS // 2
LANES = 2 * COLS
DEVS = 128


def sigmoid(x):
    return 0.5 * jnp.tanh(0.5 * x) + 0.5


def normalize(x):
    center = x - jnp.mean(x, axis=0, keepdims=True)
    spread = jnp.mean(center * center, axis=0, keepdims=True)
    return (center * lax.rsqrt(spread + 1e-05)).astype(BF16)


def tile_mask(rows_ref, cols_ref):
    row0 = lax.axis_index("row") * ROWS
    col = lax.axis_index("col")
    line = cols_ref[pl.ds(col // 2, 1), :].astype(F32)
    swapped = pltpu.roll(line, COLS, 1)
    lane = lax.broadcasted_iota(jnp.int32, (1, LANES), 1)
    low = lane < COLS
    even = (col % 2) == 0
    cols = jnp.where(low == even, line, swapped)

    def at(s):
        top = rows_ref[row0 + s].astype(F32)
        bottom = rows_ref[row0 + HALF + s].astype(F32)
        return cols * jnp.where(low, top, bottom)

    return at


def project(x, w, mask_at, s0, count, stage):
    normed = normalize(x)
    p = jnp.dot(w, normed, preferred_element_type=F32)
    mask = jnp.concatenate([mask_at(s0 + n) for n in range(count)], axis=1)
    left = mask * sigmoid(p[0:128]) * p[128:256]
    right = mask * sigmoid(p[256:384]) * p[384:512]
    for n in range(count):
        lanes = slice(n * LANES, (n + 1) * LANES)
        stage[pl.ds(s0 + n, 128, stride=2 * HALF), :] = left[:, lanes]
        stage[pl.ds(HALF + s0 + n, 128, stride=2 * HALF), :] = right[:, lanes]
    return sigmoid(p[512:640])


def put_pieces(stage, pieces_ref):
    step = 16
    for h in range(0, DEVS, step):
        block = stage[h * 2 * HALF : (h + step) * 2 * HALF, :]
        pieces_ref[h : h + step] = block.reshape(step, 2 * HALF, LANES).astype(BF16)


def first_kernel(rows_ref, cols_ref, pair_ref, w_in_ref, w_gate_ref, pieces_ref, res_ref, gate_ref, stage):
    w = jnp.concatenate([w_in_ref[...].T, w_gate_ref[...].T], axis=0)
    mask_at = tile_mask(rows_ref, cols_ref)
    for s in range(0, HALF, 2):
        x = jnp.concatenate(
            [pair_ref[s], pair_ref[HALF + s], pair_ref[s + 1], pair_ref[HALF + s + 1]], axis=0
        )
        x = x.astype(F32).T
        lanes = slice(s * LANES, (s + 2) * LANES)
        gate_ref[:, lanes] = project(x, w, mask_at, s, 2, stage)
        res_ref[:, lanes] = x
    put_pieces(stage, pieces_ref)


def product_kernel(incoming, x_ref, out_ref, left, right):
    for at, whole in ((0, left), (HALF, right)):
        for pair in range(4):
            a = x_ref[:, 2 * pair, at : at + HALF, :].reshape(16 * HALF, LANES)
            b = x_ref[:, 2 * pair + 1, at : at + HALF, :].reshape(16 * HALF, LANES)
            top = jnp.concatenate([a[:, :COLS], b[:, :COLS]], axis=1)
            bottom = jnp.concatenate([a[:, COLS:], b[:, COLS:]], axis=1)
            lanes = slice(pair * LANES, (pair + 1) * LANES)
            whole[:, 0, :, lanes] = top.reshape(16, HALF, LANES)
            whole[:, 1, :, lanes] = bottom.reshape(16, HALF, LANES)
    lhs = left[...].reshape(512, 512)
    rhs = right[...].reshape(512, 512)
    dims = (((0,), (0,)), ((), ())) if incoming else (((1,), (1,)), ((), ()))
    mixed = lax.dot_general(lhs, rhs, dims, preferred_element_type=F32).astype(BF16)
    mixed = mixed.reshape(16, 2, HALF, 512)
    for pair in range(4):
        lanes = slice(pair * LANES, (pair + 1) * LANES)
        top = mixed[:, 0, :, lanes].reshape(16 * HALF, LANES)
        bottom = mixed[:, 1, :, lanes].reshape(16 * HALF, LANES)
        a = jnp.concatenate([top[:, :COLS], bottom[:, :COLS]], axis=1)
        b = jnp.concatenate([top[:, COLS:], bottom[:, COLS:]], axis=1)
        out_ref[:, 2 * pair] = a.reshape(16, HALF, LANES)
        out_ref[:, 2 * pair + 1] = b.reshape(16, HALF, LANES)


def scale_mixed(mixed_ref, scaled):
    total = jnp.zeros((HALF, LANES), F32)
    for h in range(128):
        total += mixed_ref[h].astype(F32)
    mean = total * (1.0 / 128)
    square = jnp.zeros((HALF, LANES), F32)
    for h in range(128):
        center = mixed_ref[h].astype(F32) - mean
        square += center * center
    factor = lax.rsqrt(jnp.maximum(square * (1.0 / 128), 1.0))
    for h in range(128):
        scaled[h * HALF : (h + 1) * HALF, :] = (mixed_ref[h].astype(F32) - mean) * factor


def finish(scaled, s, w_out, res_ref, gate_ref):
    lanes = slice(s * LANES, (s + 2) * LANES)
    both = jnp.concatenate(
        [scaled[pl.ds(s + n, 128, stride=HALF), :].astype(BF16) for n in range(2)], axis=1
    )
    update = jnp.dot(w_out, both, preferred_element_type=F32)
    return (res_ref[:, lanes] + gate_ref[:, lanes] * update).astype(BF16)


def middle_kernel(
    rows_ref, cols_ref, mixed_ref, res_ref, gate_ref, w_out_ref, w_in_ref, w_gate_ref,
    pieces_ref, next_res_ref, next_gate_ref, scaled, stage,
):
    w_out = w_out_ref[...].T
    w = jnp.concatenate([w_in_ref[...].T, w_gate_ref[...].T], axis=0)
    mask_at = tile_mask(rows_ref, cols_ref)
    scale_mixed(mixed_ref, scaled)
    for s in range(0, HALF, 2):
        x = finish(scaled, s, w_out, res_ref, gate_ref).astype(F32)
        lanes = slice(s * LANES, (s + 2) * LANES)
        next_gate_ref[:, lanes] = project(x, w, mask_at, s, 2, stage)
        next_res_ref[:, lanes] = x
    put_pieces(stage, pieces_ref)


def last_kernel(mixed_ref, res_ref, gate_ref, w_out_ref, up_ref, down_ref, out_ref, scaled):
    w_out = w_out_ref[...].T
    up = up_ref[...].T
    down = down_ref[...].T
    scale_mixed(mixed_ref, scaled)
    for s in range(0, HALF, 2):
        x = finish(scaled, s, w_out, res_ref, gate_ref).astype(F32)
        p = jnp.dot(up, normalize(x), preferred_element_type=F32)
        hidden = (p[:512] * sigmoid(p[:512]) * p[512:]).astype(BF16)
        y = x + jnp.dot(down, hidden, preferred_element_type=F32)
        y = y.T.astype(BF16)
        for n, at in enumerate((s, HALF + s, s + 1, HALF + s + 1)):
            out_ref[at] = y[n * COLS : (n + 1) * COLS]


SMEM = pl.BlockSpec(memory_space=pltpu.SMEM)
VMEM = pl.BlockSpec(memory_space=pltpu.VMEM)
PARAMS = pltpu.CompilerParams(vmem_limit_bytes=32 << 20)


def exchange(x):
    return lax.all_to_all(x, ("row", "col"), 0, 0, tiled=True)


def on_device(
    pair, residue_mask, out_in_w, out_gate_w, out_out_w, inc_in_w, inc_gate_w, inc_out_w,
    trans_up, trans_down,
):
    mask_cols = residue_mask.reshape(4, 128)
    pieces_t = jax.ShapeDtypeStruct((DEVS, 2 * HALF, LANES), BF16)
    mixed_t = jax.ShapeDtypeStruct((16, 8, HALF, LANES), BF16)
    wide_t = jax.ShapeDtypeStruct((CHANS, ROWS * COLS), F32)
    stage_t = pltpu.VMEM((DEVS * 2 * HALF, LANES), F32)
    scaled_t = pltpu.VMEM((DEVS * HALF, LANES), F32)
    whole_t = pltpu.VMEM((16, 2, HALF, 512), BF16)

    def product(incoming, pieces):
        mixed = pl.pallas_call(
            functools.partial(product_kernel, incoming),
            out_shape=mixed_t,
            in_specs=[VMEM],
            out_specs=VMEM,
            scratch_shapes=[whole_t, whole_t],
            compiler_params=PARAMS,
        )(pieces.reshape(16, 8, 2 * HALF, LANES))
        return mixed.reshape(DEVS, HALF, LANES)

    pieces, res, gate = pl.pallas_call(
        first_kernel,
        out_shape=(pieces_t, wide_t, wide_t),
        in_specs=[SMEM] + [VMEM] * 4,
        out_specs=(VMEM,) * 3,
        scratch_shapes=[stage_t],
        compiler_params=PARAMS,
    )(residue_mask, mask_cols, pair, out_in_w, out_gate_w)
    mixed = exchange(product(False, exchange(pieces)))
    pieces, res, gate = pl.pallas_call(
        middle_kernel,
        out_shape=(pieces_t, wide_t, wide_t),
        in_specs=[SMEM] + [VMEM] * 7,
        out_specs=(VMEM,) * 3,
        scratch_shapes=[scaled_t, stage_t],
        compiler_params=PARAMS,
    )(residue_mask, mask_cols, mixed, res, gate, out_out_w, inc_in_w, inc_gate_w)
    mixed = exchange(product(True, exchange(pieces)))
    return pl.pallas_call(
        last_kernel,
        out_shape=jax.ShapeDtypeStruct((ROWS, COLS, CHANS), BF16),
        in_specs=[VMEM] * 6,
        out_specs=VMEM,
        scratch_shapes=[scaled_t],
        compiler_params=PARAMS,
    )(mixed, res, gate, inc_out_w, trans_up, trans_down)


def solution(mesh):
    in_specs = (P("row", "col", None), P(), P(), P(), P(), P(), P(), P(), P(), P())
    out_specs = P("row", "col", None)
    return jax.shard_map(
        on_device, mesh=mesh, in_specs=in_specs, out_specs=out_specs, check_vma=False
    )
```

time: 872 us -> 109 us (0.12)
  waiting for transfers between devices: 733 us -> 0 us
  blocking collectives: 0 us -> 88.8 us
  local copies, waits for them, and re-layouts: 60 us -> 4.09 us
  other arithmetic: 34.1 us -> 0 us
  matrix products: 23.9 us -> 0 us
  Pallas kernels: 0 us -> 15.4 us
  between operations: 13.8 us -> 0.09 us
    psum x2 -> x0, waiting for transfers between devices: 508 us -> none  [from_root(): return lax.psum(block, axis)]
    all_gather x4 -> x0, waiting for transfers between devices: 223 us -> none  [the longest x1 73.6 us: on_device(): right_rows = lax.all_gather(right, 'col', axis=2, tiled=True)]
    all_to_all x0 -> x4, blocking collectives: none -> 88.8 us  [exchange(): return lax.all_to_all(x, ('row', 'col'), 0, 0, tiled=True)]
    all_gather x3 -> x0, local copies, waits for them, and re-layouts: 45.3 us -> none  [the longest x1 23.8 us: on_device(): lax.all_gather(right, 'row', axis=1, tiled=True)]
    dot_general x10 -> x0, matrix products: 23.9 us -> none  [the longest x1 9.67 us: on_device(): jnp.einsum('hki,hkj->hij', left_cols, right_all, preferred_element_type=j...]
    pallas_call x0 -> x5, Pallas kernels: none -> 15.4 us  [the longest x1 6.58 us: on_device(): pl.pallas_call(last_kernel, out_shape=jax.ShapeDtypeStruct((ROWS, COLS, C...]
    select_n x2 -> x0, other arithmetic: 13.3 us -> none  [from_root(): jnp.where(lax.axis_index(axis) == holder, block, jnp.zeros_like(block))]
    concatenate x1 -> x0, local copies, waits for them, and re-layouts: 12.5 us -> none  [on_device(): jnp.concatenate([from_root(right_rows, 'row', 2 * col_idx + which) for wh...]
  transfers between devices with their start and end apart: 6 -> 0, of which waited for: 6 -> 0; matrix products, arithmetic and copies ran while one was open for 7% -> 0% of each run, Pallas kernels for 0% -> 0%
where the time goes in v1:
time: 109 us; the launch traced here: 108 us
  blocking collectives  88.8 us (81%)
  Pallas kernels  15.4 us (14%)
  local copies, waits for them, and re-layouts  4.09 us (4%)
    all_to_all x4, blocking collectives, exchange(): return lax.all_to_all(x, ('row', 'col'), 0, 0, tiled=True)  88.8 us
    pallas_call x1, Pallas kernels, on_device(): pl.pallas_call(last_kernel, out_shape=jax.ShapeDtypeStruct((ROWS, COLS, C...  6.58 us
    unnamed x22, local copies, waits for them, and re-layouts  4.09 us
    pallas_call x1, Pallas kernels, on_device(): pl.pallas_call(middle_kernel, out_shape=(pieces_t, wide_t, wide_t), in_sp...  4.08 us
    pallas_call x1, Pallas kernels, on_device(): pl.pallas_call(first_kernel, out_shape=(pieces_t, wide_t, wide_t), in_spe...  2.97 us

profile of v1, /device:TPU:1, one launch (start us, length us, event | category | flops | bytes accessed | tf_op | source)
XLA Modules:
  0.0 108.4 jit_solution(5735820660234363785)
XLA Ops:
  0.0 0.0 copy-start
  0.0 1.0 copy-done
  1.0 0.0 copy-start.4
  1.0 0.9 copy-done.4
  1.9 0.0 copy-start.8
  1.9 0.8 copy-done.8
  2.7 0.0 copy-start.9
  2.7 0.7 copy-done.9
  3.4 3.0 %shard_map.100 = (bf16[128,32,128]{2,1,0:T(8,128)(2,1)S(1)}, f32[128,2048]{1,0:T(8,128)S(1)}, f32[128,2048]{1,0:T(8,128)S(1)}) custom-call(s32[512]{0:T(512)S(1)} %copy-done.9, s32[4,128]{1,0:T(4,128)S(1)} %bitcast.9, bf16[32,64,128]{2,1,0:T(8,128)(2,1)S(1)} %copy-done, bf16[128,512]{1,0:T(8,128)(2,1)S(1)} %copy-done.4, bf16[128,128]{1,0:T(8,128)(2,1)S(1)} %copy-done.8), custom_call_target="tpu_custom_call" | custom-call | tf_op jit(solution)/shard_map/pallas_call | solution.py:191
  6.4 30.9 %all_to_all.20 = bf16[128,32,128]{2,1,0:T(8,128)(2,1)S(1)} all-to-all(bf16[128,32,128]{2,1,0:T(8,128)(2,1)S(1)} %get-tuple-element.11), channel_id=1, replica_groups=mesh['row'=16,'col'=8] {'row','col'}, dimensions={0} | all-to-all | bytes 2097152 | tf_op jit(solution)/shard_map/all_to_all | solution.py:165
  37.3 0.7 shard_map.101
  38.0 0.0 copy-start.3
  38.0 0.0 copy-start.5
  38.0 0.0 copy-start.6
  38.0 17.3 %all_to_all.21.mixed_ref = bf16[128,16,128]{2,1,0:T(8,128)(2,1)S(1)} all-to-all(bf16[128,16,128]{2,1,0:T(8,128)(2,1)S(1)} %bitcast.7), channel_id=1, replica_groups=mesh['row'=16,'col'=8] {'row','col'}, dimensions={0} | all-to-all | bytes 1048576 | tf_op jit(solution)/shard_map/all_to_all | solution.py:165
  55.3 0.0 copy-start.10
  55.3 0.0 copy-done.3
  55.3 0.0 copy-done.5
  55.3 0.0 copy-done.6
  55.3 0.7 copy-done.10
  56.0 4.1 %shard_map.102 = (bf16[128,32,128]{2,1,0:T(8,128)(2,1)S(1)}, f32[128,2048]{1,0:T(8,128)S(1)}, f32[128,2048]{1,0:T(8,128)S(1)}) custom-call(s32[512]{0:T(512)S(1)} %copy-done.10, s32[4,128]{1,0:T(4,128)S(1)} %bitcast.10, bf16[128,16,128]{2,1,0:T(8,128)(2,1)S(1)} %all_to_all.21.mixed_ref, f32[128,2048]{1,0:T(8,128)S(1)} %get-tuple-element.12.res_ref, ...), custom_call_target="tpu_custom_call" | custom-call | tf_op jit(solution)/shard_map/pallas_call | solution.py:200
  60.1 23.3 %all_to_all.22 = bf16[128,32,128]{2,1,0:T(8,128)(2,1)S(1)} all-to-all(bf16[128,32,128]{2,1,0:T(8,128)(2,1)S(1)} %get-tuple-element.14), channel_id=1, replica_groups=mesh['row'=16,'col'=8] {'row','col'}, dimensions={0} | all-to-all | bytes 2097152 | tf_op jit(solution)/shard_map/all_to_all | solution.py:165
  83.4 1.1 shard_map.103
  84.4 0.0 copy-start.1
  84.5 0.0 copy-start.2
  84.5 0.0 copy-start.7
  84.5 17.3 %all_to_all.23.mixed_ref = bf16[128,16,128]{2,1,0:T(8,128)(2,1)S(1)} all-to-all(bf16[128,16,128]{2,1,0:T(8,128)(2,1)S(1)} %bitcast.8), channel_id=1, replica_groups=mesh['row'=16,'col'=8] {'row','col'}, dimensions={0} | all-to-all | bytes 1048576 | tf_op jit(solution)/shard_map/all_to_all | solution.py:165
  101.8 0.0 copy-done.1
  101.8 0.0 copy-done.2
  101.8 0.0 copy-done.7
  101.8 6.6 %shard_map.104 = bf16[32,64,128]{2,1,0:T(8,128)(2,1)} custom-call(bf16[128,16,128]{2,1,0:T(8,128)(2,1)S(1)} %all_to_all.23.mixed_ref, f32[128,2048]{1,0:T(8,128)S(1)} %get-tuple-element.15.res_ref, f32[128,2048]{1,0:T(8,128)S(1)} %get-tuple-element.16.gate_ref, bf16[128,128]{1,0:T(8,128)(2,1)S(1)} %copy-done.7, bf16[128,1024]{1,0:T(8,128)(2,1)S(1)} %copy-done.1, ...), custom_call_target="tpu_custom_call" | custom-call | tf_op jit(solution)/shard_map/pallas_call | solution.py:209
Async XLA Ops:
  0.0 1.0 copy-start
  1.0 0.9 copy-start.4
  1.9 0.8 copy-start.8
  2.7 0.7 copy-start.9
  38.0 17.3 %copy-start.3 = (bf16[128,512]{1,0:T(8,128)(2,1)S(1)}, bf16[128,512]{1,0:T(8,128)(2,1)}, u32[]{:S(2)}) copy-start(bf16[128,512]{1,0:T(8,128)(2,1)} %w_in_ref.3) | copy-start | bytes 393220
  38.0 17.3 %copy-start.5 = (bf16[128,128]{1,0:T(8,128)(2,1)S(1)}, bf16[128,128]{1,0:T(8,128)(2,1)}, u32[]{:S(2)}) copy-start(bf16[128,128]{1,0:T(8,128)(2,1)} %w_out_ref.2) | copy-start | bytes 98308
  38.0 17.3 %copy-start.6 = (bf16[128,128]{1,0:T(8,128)(2,1)S(1)}, bf16[128,128]{1,0:T(8,128)(2,1)}, u32[]{:S(2)}) copy-start(bf16[128,128]{1,0:T(8,128)(2,1)} %w_gate_ref.3) | copy-start | bytes 98308
  55.3 0.7 copy-start.10
  84.4 17.3 %copy-start.1 = (bf16[128,1024]{1,0:T(8,128)(2,1)S(1)}, bf16[128,1024]{1,0:T(8,128)(2,1)}, u32[]{:S(2)}) copy-start(bf16[128,1024]{1,0:T(8,128)(2,1)} %up_ref.1) | copy-start | bytes 786436
  84.5 17.3 %copy-start.2 = (bf16[512,128]{1,0:T(8,128)(2,1)S(1)}, bf16[512,128]{1,0:T(8,128)(2,1)}, u32[]{:S(2)}) copy-start(bf16[512,128]{1,0:T(8,128)(2,1)} %down_ref.1) | copy-start | bytes 393220
  84.5 17.3 %copy-start.7 = (bf16[128,128]{1,0:T(8,128)(2,1)S(1)}, bf16[128,128]{1,0:T(8,128)(2,1)}, u32[]{:S(2)}) copy-start(bf16[128,128]{1,0:T(8,128)(2,1)} %w_out_ref.3) | copy-start | bytes 98308

commit v2 on v1

v2 whole, which is shorter than its diff:
```python
import functools

import jax
import jax.numpy as jnp
from jax import lax
from jax.experimental import pallas as pl
from jax.experimental.pallas import tpu as pltpu
from jax.sharding import PartitionSpec as P

F32 = jnp.float32
BF16 = jnp.bfloat16
ROWS, COLS, CHANS = 32, 64, 128
HALF = ROWS // 2
LANES = 2 * COLS
SPOTS = ROWS * COLS
DEVS = 128
STAGE = 40
SCALED = 24


def tree(parts):
    while len(parts) > 1:
        parts = [a + b for a, b in zip(parts[::2], parts[1::2])]
    return parts[0]


def normalize(x):
    center = x - jnp.mean(x, axis=0, keepdims=True)
    spread = jnp.mean(center * center, axis=0, keepdims=True)
    return (center * lax.rsqrt(spread + 1e-05)).astype(BF16)


def put_mask(rows_ref, cols_ref, mask_ref):
    row0 = lax.axis_index("row") * ROWS
    col = lax.axis_index("col")
    line = cols_ref[pl.ds(col // 2, 1), :].astype(F32)
    swapped = pltpu.roll(line, COLS, 1)
    low = lax.broadcasted_iota(jnp.int32, (1, LANES), 1) < COLS
    cols = jnp.where(low == ((col % 2) == 0), line, swapped)
    for s in range(HALF):
        top = rows_ref[row0 + s].astype(F32)
        bottom = rows_ref[row0 + HALF + s].astype(F32)
        mask_ref[s : s + 1, :] = cols * jnp.where(low, top, bottom)


def project(x, w):
    return jnp.dot(w, normalize(x), preferred_element_type=F32)


def stage_operands(p, mask_ref, s0, count, stage):
    mask = jnp.concatenate([mask_ref[s0 + n : s0 + n + 1, :] for n in range(count)], axis=1)
    half_mask = 0.5 * mask
    for at, k in ((0, 0), (HALF, 256)):
        value = half_mask * p[k + 128 : k + 256]
        value = value * jnp.tanh(0.5 * p[k : k + 128]) + value
        for n in range(count):
            stage[pl.ds(at + s0 + n, DEVS, stride=STAGE), :] = value[:, n * LANES : (n + 1) * LANES]


def put_pieces(stage, pieces_ref):
    for h in range(DEVS):
        pieces_ref[h] = stage[h * STAGE : h * STAGE + 2 * HALF, :].astype(BF16)


def load_steps(pair_ref, s0, count):
    blocks = []
    for s in range(s0, s0 + count):
        blocks += [pair_ref[s], pair_ref[HALF + s]]
    return jnp.concatenate(blocks, axis=0).T


def first_kernel(
    rows_hbm, cols_hbm, pair_hbm, w_in_hbm, pieces_ref, mask_ref,
    rows_ref, cols_ref, pair_ref, w_in_ref, stage, sems,
):
    moves = ((pair_hbm, pair_ref), (w_in_hbm, w_in_ref), (cols_hbm, cols_ref), (rows_hbm, rows_ref))
    copies = [pltpu.make_async_copy(a, b, sems.at[n]) for n, (a, b) in enumerate(moves)]
    for copy in copies:
        copy.start()
    for copy in copies:
        copy.wait()
    put_mask(rows_ref, cols_ref, mask_ref)
    w = w_in_ref[...].T
    for s in range(0, HALF, 8):
        p = project(load_steps(pair_ref, s, 8).astype(F32), w)
        stage_operands(p, mask_ref, s, 8, stage)
    put_pieces(stage, pieces_ref)


def gate_kernel(from_pair, x_ref, w_gate_ref, gate_ref, *res_ref):
    w = w_gate_ref[...].T
    for s in range(0, HALF, 8):
        lanes = slice(s * LANES, (s + 8) * LANES)
        if from_pair:
            x = load_steps(x_ref, s, 8)
            res_ref[0][:, lanes] = x
        else:
            x = x_ref[:, lanes]
        gate_ref[:, lanes] = 0.5 * jnp.tanh(0.5 * project(x.astype(F32), w)) + 0.5


def product_kernel(incoming, x_ref, out_ref, left, right):
    for at, whole in ((0, left), (HALF, right)):
        for pair in range(4):
            a = x_ref[:, 2 * pair, at : at + HALF, :].reshape(16 * HALF, LANES)
            b = x_ref[:, 2 * pair + 1, at : at + HALF, :].reshape(16 * HALF, LANES)
            top = jnp.concatenate([a[:, :COLS], b[:, :COLS]], axis=1)
            bottom = jnp.concatenate([a[:, COLS:], b[:, COLS:]], axis=1)
            lanes = slice(pair * LANES, (pair + 1) * LANES)
            whole[:, 0, :, lanes] = top.reshape(16, HALF, LANES)
            whole[:, 1, :, lanes] = bottom.reshape(16, HALF, LANES)
    lhs = left[...].reshape(512, 512)
    rhs = right[...].reshape(512, 512)
    dims = (((0,), (0,)), ((), ())) if incoming else (((1,), (1,)), ((), ()))
    mixed = lax.dot_general(lhs, rhs, dims, preferred_element_type=F32).astype(BF16)
    mixed = mixed.reshape(16, 2, HALF, 512)
    for pair in range(4):
        lanes = slice(pair * LANES, (pair + 1) * LANES)
        top = mixed[:, 0, :, lanes].reshape(16 * HALF, LANES)
        bottom = mixed[:, 1, :, lanes].reshape(16 * HALF, LANES)
        a = jnp.concatenate([top[:, :COLS], bottom[:, :COLS]], axis=1)
        b = jnp.concatenate([top[:, COLS:], bottom[:, COLS:]], axis=1)
        out_ref[:, 2 * pair] = a.reshape(16, HALF, LANES)
        out_ref[:, 2 * pair + 1] = b.reshape(16, HALF, LANES)


def scale_mixed(mixed_ref, scaled):
    sums = [None] * 8
    for h in range(DEVS):
        value = mixed_ref[h].astype(F32)
        sums[h % 8] = value if h < 8 else sums[h % 8] + value
    mean = tree(sums) * (1.0 / 128)
    for h in range(DEVS):
        center = mixed_ref[h].astype(F32) - mean
        sums[h % 8] = center * center if h < 8 else sums[h % 8] + center * center
    factor = lax.rsqrt(jnp.maximum(tree(sums) * (1.0 / 128), 1.0))
    for h in range(DEVS):
        scaled[h * SCALED : h * SCALED + HALF, :] = (mixed_ref[h].astype(F32) - mean) * factor


def finish(scaled, s0, count, w_out, res_ref, gate_ref):
    lanes = slice(s0 * LANES, (s0 + count) * LANES)
    rows = [
        scaled[pl.ds(s0 + n, DEVS, stride=SCALED), :].astype(BF16) for n in range(count)
    ]
    update = jnp.dot(w_out, jnp.concatenate(rows, axis=1), preferred_element_type=F32)
    return (res_ref[:, lanes].astype(F32) + gate_ref[:, lanes] * update).astype(BF16)


def middle_kernel(
    mixed_ref, mask_ref, res_ref, gate_ref, w_out_ref, w_in_ref, pieces_ref, first_ref, scaled, stage
):
    w_out = w_out_ref[...].T
    w = w_in_ref[...].T
    scale_mixed(mixed_ref, scaled)
    for s in range(0, HALF, 8):
        x = finish(scaled, s, 8, w_out, res_ref, gate_ref)
        first_ref[:, s * LANES : (s + 8) * LANES] = x
        stage_operands(project(x.astype(F32), w), mask_ref, s, 8, stage)
    put_pieces(stage, pieces_ref)


def last_kernel(mixed_ref, res_ref, gate_ref, w_out_ref, up_ref, down_ref, out_ref, scaled):
    w_out = w_out_ref[...].T
    up = up_ref[...].T
    down = down_ref[...].T
    scale_mixed(mixed_ref, scaled)
    for s in range(0, HALF, 8):
        x = finish(scaled, s, 8, w_out, res_ref, gate_ref).astype(F32)
        p = project(x, up)
        half = 0.5 * p[:512]
        hidden = ((half * jnp.tanh(half) + half) * p[512:]).astype(BF16)
        y = x + jnp.dot(down, hidden, preferred_element_type=F32)
        y = y.astype(BF16).T
        for n in range(8):
            out_ref[s + n] = y[2 * n * COLS : (2 * n + 1) * COLS]
            out_ref[HALF + s + n] = y[(2 * n + 1) * COLS : (2 * n + 2) * COLS]


VMEM = pl.BlockSpec(memory_space=pltpu.VMEM)
ANY = pl.BlockSpec(memory_space=pl.ANY)
PIECES = jax.ShapeDtypeStruct((DEVS, 2 * HALF, LANES), BF16)
MASK = jax.ShapeDtypeStruct((HALF, LANES), F32)
MIXED = jax.ShapeDtypeStruct((16, 8, HALF, LANES), BF16)
GATE = jax.ShapeDtypeStruct((CHANS, SPOTS), F32)
RES = jax.ShapeDtypeStruct((CHANS, SPOTS), BF16)
TILE = jax.ShapeDtypeStruct((ROWS, COLS, CHANS), BF16)
STAGE_T = pltpu.VMEM((DEVS * STAGE, LANES), F32)
SCALED_T = pltpu.VMEM((DEVS * SCALED, LANES), F32)


def local(kernel, out, scratch, args, limit=32, flops=0, moved=0):
    return pl.pallas_call(
        kernel,
        out_shape=out,
        in_specs=[VMEM] * len(args),
        out_specs=jax.tree.map(lambda _: VMEM, out),
        scratch_shapes=scratch,
        compiler_params=pltpu.CompilerParams(vmem_limit_bytes=limit << 20),
        cost_estimate=pl.CostEstimate(flops=flops, bytes_accessed=moved, transcendentals=0),
    )(*args)


def first(residue_mask, pair, w_in):
    return pl.pallas_call(
        first_kernel,
        out_shape=(PIECES, MASK),
        in_specs=[ANY] * 4,
        out_specs=(VMEM, VMEM),
        scratch_shapes=[
            pltpu.SMEM((512,), jnp.int32),
            pltpu.VMEM((4, LANES), jnp.int32),
            pltpu.VMEM((ROWS, COLS, CHANS), BF16),
            pltpu.VMEM((CHANS, 512), BF16),
            STAGE_T,
            pltpu.SemaphoreType.DMA((4,)),
        ],
        compiler_params=pltpu.CompilerParams(vmem_limit_bytes=60 << 20),
    )(residue_mask, residue_mask.reshape(4, LANES), pair, w_in)


def gate_pair(pair, w_gate):
    kernel = functools.partial(gate_kernel, True)
    return local(kernel, (GATE, RES), [], (pair, w_gate), flops=1 << 28, moved=4 << 20)


def gate_first(x, w_gate):
    kernel = functools.partial(gate_kernel, False)
    return local(kernel, GATE, [], (x, w_gate), flops=1 << 28, moved=4 << 20)


def product(incoming, pieces):
    whole = pltpu.VMEM((16, 2, HALF, 512), BF16)
    kernel = functools.partial(product_kernel, incoming)
    mixed = local(kernel, MIXED, [whole, whole], (pieces.reshape(16, 8, 2 * HALF, LANES),))
    return mixed.reshape(DEVS, HALF, LANES)


def middle(*args):
    return local(middle_kernel, (PIECES, RES), [SCALED_T, STAGE_T], args)


def last(*args):
    return local(last_kernel, TILE, [SCALED_T], args)


def exchange(x):
    return lax.all_to_all(x, ("row", "col"), 0, 0, tiled=True)


def on_device(
    pair, residue_mask, out_in_w, out_gate_w, out_out_w, inc_in_w, inc_gate_w, inc_out_w,
    trans_up, trans_down,
):
    pieces, mask = first(residue_mask, pair, out_in_w)
    pair, pieces = lax.optimization_barrier((pair, pieces))
    gate, res = gate_pair(pair, out_gate_w)
    mixed = exchange(product(False, exchange(pieces)))
    pieces, res = middle(mixed, mask, res, gate, out_out_w, inc_in_w)
    gate = gate_first(res, inc_gate_w)
    mixed = exchange(product(True, exchange(pieces)))
    return last(mixed, res, gate, inc_out_w, trans_up, trans_down)


def solution(mesh):
    in_specs = (P("row", "col", None), P(), P(), P(), P(), P(), P(), P(), P(), P())
    out_specs = P("row", "col", None)
    return jax.shard_map(
        on_device, mesh=mesh, in_specs=in_specs, out_specs=out_specs, check_vma=False
    )
```

time: 109 us -> 102 us (0.936)
  blocking collectives: 88.8 us -> 54.4 us
  waiting for transfers between devices: 0 us -> 26.3 us
  starting transfers between devices: 0 us -> 7.37 us
  local copies, waits for them, and re-layouts: 4.09 us -> 0.05 us
  Pallas kernels: 15.4 us -> 13.3 us
    all_to_all x4 -> x2, blocking collectives: 88.8 us -> 54.4 us  [exchange(): return lax.all_to_all(x, ('row', 'col'), 0, 0, tiled=True)]
    all_to_all x0 -> x2, waiting for transfers between devices: none -> 26.3 us  [exchange(): return lax.all_to_all(x, ('row', 'col'), 0, 0, tiled=True)]
    all_to_all x0 -> x2, starting transfers between devices: none -> 7.37 us  [exchange(): return lax.all_to_all(x, ('row', 'col'), 0, 0, tiled=True)]
    unnamed x22 -> x18, local copies, waits for them, and re-layouts: 4.09 us -> 0.05 us
    pallas_call x5 -> x7, Pallas kernels: 15.4 us -> 13.3 us  [the longest x6 10.2 us: local(): pl.pallas_call(kernel, out_shape=out, in_specs=[VMEM] * len(args), out_sp...]
  transfers between devices with their start and end apart: 0 -> 2, of which waited for: 0 -> 2; matrix products, arithmetic and copies ran while one was open for 0% -> 0% of each run, Pallas kernels for 0% -> 1%
where the time goes in v2:
time: 102 us
  blocking collectives  54.4 us (53%)
  waiting for transfers between devices  26.3 us (26%)
  Pallas kernels  13.3 us (13%)
  starting transfers between devices  7.37 us (7%)
    all_to_all x2, blocking collectives, exchange(): return lax.all_to_all(x, ('row', 'col'), 0, 0, tiled=True)  54.4 us
    all_to_all x2, waiting for transfers between devices, exchange(): return lax.all_to_all(x, ('row', 'col'), 0, 0, tiled=True)  26.3 us
    pallas_call x6, Pallas kernels, local(): pl.pallas_call(kernel, out_shape=out, in_specs=[VMEM] * len(args), out_sp...  10.2 us
    all_to_all x2, starting transfers between devices, exchange(): return lax.all_to_all(x, ('row', 'col'), 0, 0, tiled=True)  7.37 us
    pallas_call x1, Pallas kernels, first(): pl.pallas_call(first_kernel, out_shape=(PIECES, MASK), in_specs=[ANY] * 4...  3.11 us
  transfers between devices with their start and end apart: 2, of which 2 were waited for; matrix products, arithmetic and copies ran while one was open for 0% of the time, Pallas kernels for 1%

profile of v2, /device:TPU:1, one launch (start us, length us, event | category | flops | bytes accessed | tf_op | source)
XLA Modules:
  0.0 101.6 jit_solution(10350057035291714451)
XLA Ops:
  0.0 3.1 %shard_map.100 = (bf16[128,32,128]{2,1,0:T(8,128)(2,1)}, f32[16,128]{1,0:T(8,128)}) custom-call(s32[512]{0:T(512)} %rows_hbm.1, s32[4,128]{1,0:T(4,128)} %bitcast.7, bf16[32,64,128]{2,1,0:T(8,128)(2,1)} %x_ref, bf16[128,512]{1,0:T(8,128)(2,1)} %w_in_hbm.1), custom_call_target="tpu_custom_call" | custom-call | tf_op jit(solution)/shard_map/pallas_call | solution.py:205
  3.1 31.1 %all_to_all.20 = bf16[128,32,128]{2,1,0:T(8,128)(2,1)S(1)} all-to-all(bf16[128,32,128]{2,1,0:T(8,128)(2,1)} %get-tuple-element.14), channel_id=1, replica_groups=mesh['row'=16,'col'=8] {'row','col'}, dimensions={0} | all-to-all | bytes 2097152 | tf_op jit(solution)/shard_map/all_to_all | solution.py:248
  34.2 1.5 %shard_map.101 = bf16[16,8,16,128]{3,2,1,0:T(8,128)(2,1)} custom-call(bf16[16,8,32,128]{3,2,1,0:T(8,128)(2,1)S(1)} %bitcast.5), custom_call_target="tpu_custom_call" | custom-call | tf_op jit(solution)/shard_map/pallas_call | solution.py:193
  35.7 0.0 copy-start
  35.7 0.0 copy-start.8
  35.7 3.7 %all-to-all-start.1 = ((bf16[128,16,128]{2,1,0:T(8,128)(2,1)}), bf16[128,16,128]{2,1,0:T(8,128)(2,1)S(1)}, u32[]{:S(2)}, u32[]{:S(2)}) async-start(bf16[128,16,128]{2,1,0:T(8,128)(2,1)} %bitcast.2), calls=%async_computation.1 | async-start | bytes 1048576 | tf_op jit(solution)/shard_map/all_to_all | solution.py:248
  39.4 0.0 copy-done
  39.4 0.0 copy-done.8
  39.4 0.0 copy-start.2
  39.5 0.0 copy-start.4
  39.5 0.0 copy-start.7
  39.5 0.6 shard_map.102
  40.1 13.1 %all-to-all-done.1.mixed_ref = bf16[128,16,128]{2,1,0:T(8,128)(2,1)S(1)} async-done(((bf16[128,16,128]{2,1,0:T(8,128)(2,1)}), bf16[128,16,128]{2,1,0:T(8,128)(2,1)S(1)}, u32[]{:S(2)}, u32[]{:S(2)}) %all-to-all-start.1) | async-done | bytes 524320 | tf_op jit(solution)/shard_map/all_to_all | solution.py:248
  53.2 0.0 copy-done.2
  53.2 0.0 copy-done.4
  53.2 0.0 copy-done.7
  53.2 1.9 %shard_map.103 = (bf16[128,32,128]{2,1,0:T(8,128)(2,1)S(1)}, bf16[128,2048]{1,0:T(8,128)(2,1)S(1)}) custom-call(bf16[128,16,128]{2,1,0:T(8,128)(2,1)S(1)} %all-to-all-done.1.mixed_ref, f32[16,128]{1,0:T(8,128)S(1)} %copy-done.7, bf16[128,2048]{1,0:T(8,128)(2,1)S(1)} %get-tuple-element.17.res_ref, f32[128,2048]{1,0:T(8,128)S(1)} %get-tuple-element.18.gate_ref, ...), custom_call_target="tpu_custom_call" | custom-call | tf_op jit(solution)/shard_map/pallas_call | solution.py:193
  55.2 23.3 %all_to_all.21 = bf16[128,32,128]{2,1,0:T(8,128)(2,1)S(1)} all-to-all(bf16[128,32,128]{2,1,0:T(8,128)(2,1)S(1)} %get-tuple-element.19), channel_id=1, replica_groups=mesh['row'=16,'col'=8] {'row','col'}, dimensions={0} | all-to-all | bytes 2097152 | tf_op jit(solution)/shard_map/all_to_all | solution.py:248
  78.5 1.9 %shard_map.104 = bf16[16,8,16,128]{3,2,1,0:T(8,128)(2,1)} custom-call(bf16[16,8,32,128]{3,2,1,0:T(8,128)(2,1)S(1)} %bitcast.6), custom_call_target="tpu_custom_call" | custom-call | tf_op jit(solution)/shard_map/pallas_call | solution.py:193
  80.3 0.0 copy-start.6
  80.3 3.7 %all-to-all-start.3 = ((bf16[128,16,128]{2,1,0:T(8,128)(2,1)}), bf16[128,16,128]{2,1,0:T(8,128)(2,1)S(1)}, u32[]{:S(2)}, u32[]{:S(2)}) async-start(bf16[128,16,128]{2,1,0:T(8,128)(2,1)} %bitcast.4), calls=%async_computation.3 | async-start | bytes 1048576 | tf_op jit(solution)/shard_map/all_to_all | solution.py:248
  84.0 0.0 copy-done.6
  84.0 0.0 copy-start.1
  84.0 0.0 copy-start.3
  84.0 0.0 copy-start.5
  84.1 0.5 shard_map.105.gate_ref
  84.6 13.2 %all-to-all-done.3.mixed_ref = bf16[128,16,128]{2,1,0:T(8,128)(2,1)S(1)} async-done(((bf16[128,16,128]{2,1,0:T(8,128)(2,1)}), bf16[128,16,128]{2,1,0:T(8,128)(2,1)S(1)}, u32[]{:S(2)}, u32[]{:S(2)}) %all-to-all-start.3) | async-done | bytes 524320 | tf_op jit(solution)/shard_map/all_to_all | solution.py:248
  97.8 0.0 copy-done.1
  97.8 0.0 copy-done.3
  97.8 0.0 copy-done.5
  97.8 3.8 %shard_map.106 = bf16[32,64,128]{2,1,0:T(8,128)(2,1)} custom-call(bf16[128,16,128]{2,1,0:T(8,128)(2,1)S(1)} %all-to-all-done.3.mixed_ref, bf16[128,2048]{1,0:T(8,128)(2,1)S(1)} %get-tuple-element.20.x_ref.res_ref, f32[128,2048]{1,0:T(8,128)S(1)} %shard_map.105.gate_ref, bf16[128,128]{1,0:T(8,128)(2,1)S(1)} %copy-done.5, bf16[128,1024]{1,0:T(8,128)(2,1)S(1)} %copy-done.1, ...), custom_call_target="tpu_custom_call" | custom-call | tf_op jit(solution)/shard_map/pallas_call | solution.py:193
Async XLA Ops:
  35.7 3.7 %copy-start = (bf16[32,64,128]{2,1,0:T(8,128)(2,1)S(1)}, bf16[32,64,128]{2,1,0:T(8,128)(2,1)}, u32[]{:S(2)}) copy-start(bf16[32,64,128]{2,1,0:T(8,128)(2,1)} %x_ref) | copy-start | bytes 1572868
  35.7 3.7 %copy-start.8 = (bf16[128,128]{1,0:T(8,128)(2,1)S(1)}, bf16[128,128]{1,0:T(8,128)(2,1)}, u32[]{:S(2)}) copy-start(bf16[128,128]{1,0:T(8,128)(2,1)} %w_gate_ref.2) | copy-start | bytes 98308
  35.7 17.5 %all-to-all-start.1 = ((bf16[128,16,128]{2,1,0:T(8,128)(2,1)}), bf16[128,16,128]{2,1,0:T(8,128)(2,1)S(1)}, u32[]{:S(2)}, u32[]{:S(2)}) async-start(bf16[128,16,128]{2,1,0:T(8,128)(2,1)} %bitcast.2), calls=%async_computation.1 | async-start | bytes 1048576 | tf_op jit(solution)/shard_map/all_to_all | solution.py:248
  39.4 13.8 %copy-start.2 = (bf16[128,512]{1,0:T(8,128)(2,1)S(1)}, bf16[128,512]{1,0:T(8,128)(2,1)}, u32[]{:S(2)}) copy-start(bf16[128,512]{1,0:T(8,128)(2,1)} %w_in_ref.1) | copy-start | bytes 393220
  39.5 13.8 %copy-start.4 = (bf16[128,128]{1,0:T(8,128)(2,1)S(1)}, bf16[128,128]{1,0:T(8,128)(2,1)}, u32[]{:S(2)}) copy-start(bf16[128,128]{1,0:T(8,128)(2,1)} %w_out_ref.2) | copy-start | bytes 98308
  39.5 13.8 %copy-start.7 = (f32[16,128]{1,0:T(8,128)S(1)}, f32[16,128]{1,0:T(8,128)}, u32[]{:S(2)}) copy-start(f32[16,128]{1,0:T(8,128)} %get-tuple-element.15.mask_ref) | copy-start | bytes 24580
  80.3 3.7 %copy-start.6 = (bf16[128,128]{1,0:T(8,128)(2,1)S(1)}, bf16[128,128]{1,0:T(8,128)(2,1)}, u32[]{:S(2)}) copy-start(bf16[128,128]{1,0:T(8,128)(2,1)} %w_gate_ref.3) | copy-start | bytes 98308
  80.3 17.5 %all-to-all-start.3 = ((bf16[128,16,128]{2,1,0:T(8,128)(2,1)}), bf16[128,16,128]{2,1,0:T(8,128)(2,1)S(1)}, u32[]{:S(2)}, u32[]{:S(2)}) async-start(bf16[128,16,128]{2,1,0:T(8,128)(2,1)} %bitcast.4), calls=%async_computation.3 | async-start | bytes 1048576 | tf_op jit(solution)/shard_map/all_to_all | solution.py:248
  84.0 13.8 %copy-start.1 = (bf16[128,1024]{1,0:T(8,128)(2,1)S(1)}, bf16[128,1024]{1,0:T(8,128)(2,1)}, u32[]{:S(2)}) copy-start(bf16[128,1024]{1,0:T(8,128)(2,1)} %up_ref.1) | copy-start | bytes 786436
  84.0 13.8 %copy-start.3 = (bf16[512,128]{1,0:T(8,128)(2,1)S(1)}, bf16[512,128]{1,0:T(8,128)(2,1)}, u32[]{:S(2)}) copy-start(bf16[512,128]{1,0:T(8,128)(2,1)} %down_ref.1) | copy-start | bytes 393220
  84.0 13.8 %copy-start.5 = (bf16[128,128]{1,0:T(8,128)(2,1)S(1)}, bf16[128,128]{1,0:T(8,128)(2,1)}, u32[]{:S(2)}) copy-start(bf16[128,128]{1,0:T(8,128)(2,1)} %w_out_ref.3) | copy-start | bytes 98308

commit v3 on v2

--- a/solution.py
+++ b/solution.py
@@ -30,17 +30,23 @@
     return (center * lax.rsqrt(spread + 1e-05)).astype(BF16)
 
 
-def put_mask(rows_ref, cols_ref, mask_ref):
+def sigmoid(x):
+    return 0.5 * jnp.tanh(0.5 * x) + 0.5
+
+
+def put_mask(present_ref, mask_ref):
     row0 = lax.axis_index("row") * ROWS
     col = lax.axis_index("col")
-    line = cols_ref[pl.ds(col // 2, 1), :].astype(F32)
-    swapped = pltpu.roll(line, COLS, 1)
-    low = lax.broadcasted_iota(jnp.int32, (1, LANES), 1) < COLS
-    cols = jnp.where(low == ((col % 2) == 0), line, swapped)
-    for s in range(HALF):
-        top = rows_ref[row0 + s].astype(F32)
-        bottom = rows_ref[row0 + HALF + s].astype(F32)
-        mask_ref[s : s + 1, :] = cols * jnp.where(low, top, bottom)
+    lane = lax.broadcasted_iota(jnp.int32, (HALF, LANES), 1)
+    step = lax.broadcasted_iota(jnp.int32, (HALF, LANES), 0)
+    low = lane < COLS
+    line = present_ref[pl.ds(col // 2, 1), :].astype(F32)
+    cols = jnp.where(low == ((col % 2) == 0), line, pltpu.roll(line, COLS, 1))
+    line = present_ref[pl.ds(row0 // LANES, 1), :].astype(F32)
+    spot = lane - row0 % LANES
+    top = jnp.sum(jnp.where(spot == step, line, 0.0), axis=1, keepdims=True)
+    bottom = jnp.sum(jnp.where(spot == step + HALF, line, 0.0), axis=1, keepdims=True)
+    mask_ref[...] = cols * jnp.where(low, top, bottom)
 
 
 def project(x, w):
@@ -70,16 +76,15 @@
 
 
 def first_kernel(
-    rows_hbm, cols_hbm, pair_hbm, w_in_hbm, pieces_ref, mask_ref,
-    rows_ref, cols_ref, pair_ref, w_in_ref, stage, sems,
-):
-    moves = ((pair_hbm, pair_ref), (w_in_hbm, w_in_ref), (cols_hbm, cols_ref), (rows_hbm, rows_ref))
+    pair_hbm, w_in_hbm, present_hbm, pieces_ref, mask_ref, pair_ref, w_in_ref, present_ref, stage, sems
+):
+    moves = ((pair_hbm, pair_ref), (w_in_hbm, w_in_ref), (present_hbm, present_ref))
     copies = [pltpu.make_async_copy(a, b, sems.at[n]) for n, (a, b) in enumerate(moves)]
     for copy in copies:
         copy.start()
     for copy in copies:
         copy.wait()
-    put_mask(rows_ref, cols_ref, mask_ref)
+    put_mask(present_ref, mask_ref)
     w = w_in_ref[...].T
     for s in range(0, HALF, 8):
         p = project(load_steps(pair_ref, s, 8).astype(F32), w)
@@ -87,16 +92,22 @@
     put_pieces(stage, pieces_ref)
 
 
-def gate_kernel(from_pair, x_ref, w_gate_ref, gate_ref, *res_ref):
-    w = w_gate_ref[...].T
+def side_kernel(
+    pair_ref, gate_w_ref, out_w_ref, in_w_ref, next_gate_w_ref, next_out_w_ref, up_ref, down_ref,
+    gate_ref, res_ref, out_t_ref, in_t_ref, next_out_t_ref, up_t_ref, down_t_ref,
+):
+    w = gate_w_ref[...].T
     for s in range(0, HALF, 8):
         lanes = slice(s * LANES, (s + 8) * LANES)
-        if from_pair:
-            x = load_steps(x_ref, s, 8)
-            res_ref[0][:, lanes] = x
-        else:
-            x = x_ref[:, lanes]
-        gate_ref[:, lanes] = 0.5 * jnp.tanh(0.5 * project(x.astype(F32), w)) + 0.5
+        x = load_steps(pair_ref, s, 8)
+        res_ref[:, lanes] = x
+        gate_ref[:, lanes] = sigmoid(project(x.astype(F32), w))
+    out_t_ref[...] = out_w_ref[...].T
+    in_t_ref[:512] = in_w_ref[...].T
+    in_t_ref[512:] = next_gate_w_ref[...].T
+    next_out_t_ref[...] = next_out_w_ref[...].T
+    up_t_ref[...] = up_ref[...].T
+    down_t_ref[...] = down_ref[...].T
 
 
 def product_kernel(incoming, x_ref, out_ref, left, right):
@@ -148,33 +159,31 @@
 
 
 def middle_kernel(
-    mixed_ref, mask_ref, res_ref, gate_ref, w_out_ref, w_in_ref, pieces_ref, first_ref, scaled, stage
-):
-    w_out = w_out_ref[...].T
-    w = w_in_ref[...].T
+    mixed_ref, mask_ref, res_ref, gate_ref, w_out_ref, w_in_ref,
+    pieces_ref, first_ref, next_gate_ref, scaled, stage,
+):
     scale_mixed(mixed_ref, scaled)
     for s in range(0, HALF, 8):
-        x = finish(scaled, s, 8, w_out, res_ref, gate_ref)
-        first_ref[:, s * LANES : (s + 8) * LANES] = x
-        stage_operands(project(x.astype(F32), w), mask_ref, s, 8, stage)
+        lanes = slice(s * LANES, (s + 8) * LANES)
+        x = finish(scaled, s, 8, w_out_ref[...], res_ref, gate_ref)
+        first_ref[:, lanes] = x
+        p = project(x.astype(F32), w_in_ref[...])
+        stage_operands(p, mask_ref, s, 8, stage)
+        next_gate_ref[:, lanes] = sigmoid(p[512:])
     put_pieces(stage, pieces_ref)
 
 
 def last_kernel(mixed_ref, res_ref, gate_ref, w_out_ref, up_ref, down_ref, out_ref, scaled):
-    w_out = w_out_ref[...].T
-    up = up_ref[...].T
-    down = down_ref[...].T
     scale_mixed(mixed_ref, scaled)
-    for s in range(0, HALF, 8):
-        x = finish(scaled, s, 8, w_out, res_ref, gate_ref).astype(F32)
-        p = project(x, up)
-        half = 0.5 * p[:512]
-        hidden = ((half * jnp.tanh(half) + half) * p[512:]).astype(BF16)
-        y = x + jnp.dot(down, hidden, preferred_element_type=F32)
-        y = y.astype(BF16).T
-        for n in range(8):
-            out_ref[s + n] = y[2 * n * COLS : (2 * n + 1) * COLS]
-            out_ref[HALF + s + n] = y[(2 * n + 1) * COLS : (2 * n + 2) * COLS]
+    x = finish(scaled, 0, HALF, w_out_ref[...], res_ref, gate_ref).astype(F32)
+    p = project(x, up_ref[...])
+    half = (0.5 * p[:512]).astype(BF16)
+    hidden = (half * jnp.tanh(half) + half) * p[512:].astype(BF16)
+    y = x + jnp.dot(down_ref[...], hidden, preferred_element_type=F32)
+    y = y.astype(BF16).T
+    for s in range(HALF):
+        out_ref[s] = y[2 * s * COLS : (2 * s + 1) * COLS]
+        out_ref[HALF + s] = y[(2 * s + 1) * COLS : (2 * s + 2) * COLS]
 
 
 VMEM = pl.BlockSpec(memory_space=pltpu.VMEM)
@@ -205,28 +214,26 @@
     return pl.pallas_call(
         first_kernel,
         out_shape=(PIECES, MASK),
-        in_specs=[ANY] * 4,
+        in_specs=[ANY] * 3,
         out_specs=(VMEM, VMEM),
         scratch_shapes=[
-            pltpu.SMEM((512,), jnp.int32),
-            pltpu.VMEM((4, LANES), jnp.int32),
             pltpu.VMEM((ROWS, COLS, CHANS), BF16),
             pltpu.VMEM((CHANS, 512), BF16),
+            pltpu.VMEM((4, LANES), jnp.int32),
             STAGE_T,
-            pltpu.SemaphoreType.DMA((4,)),
+            pltpu.SemaphoreType.DMA((3,)),
         ],
         compiler_params=pltpu.CompilerParams(vmem_limit_bytes=60 << 20),
-    )(residue_mask, residue_mask.reshape(4, LANES), pair, w_in)
-
-
-def gate_pair(pair, w_gate):
-    kernel = functools.partial(gate_kernel, True)
-    return local(kernel, (GATE, RES), [], (pair, w_gate), flops=1 << 28, moved=4 << 20)
-
-
-def gate_first(x, w_gate):
-    kernel = functools.partial(gate_kernel, False)
-    return local(kernel, GATE, [], (x, w_gate), flops=1 << 28, moved=4 << 20)
+    )(pair, w_in, residue_mask.reshape(4, LANES))
+
+
+def weight(rows, cols=CHANS):
+    return jax.ShapeDtypeStruct((rows, cols), BF16)
+
+
+def side(*args):
+    out = (GATE, RES, weight(128), weight(640), weight(128), weight(1024), weight(128, 512))
+    return local(side_kernel, out, [], args, flops=1 << 28, moved=6 << 20)
 
 
 def product(incoming, pieces):
@@ -237,7 +244,7 @@
 
 
 def middle(*args):
-    return local(middle_kernel, (PIECES, RES), [SCALED_T, STAGE_T], args)
+    return local(middle_kernel, (PIECES, RES, GATE), [SCALED_T, STAGE_T], args)
 
 
 def last(*args):
@@ -254,12 +261,13 @@
 ):
     pieces, mask = first(residue_mask, pair, out_in_w)
     pair, pieces = lax.optimization_barrier((pair, pieces))
-    gate, res = gate_pair(pair, out_gate_w)
-    mixed = exchange(product(False, exchange(pieces)))
-    pieces, res = middle(mixed, mask, res, gate, out_out_w, inc_in_w)
-    gate = gate_first(res, inc_gate_w)
+    beside = side(pair, out_gate_w, out_out_w, inc_in_w, inc_gate_w, inc_out_w, trans_up, trans_down)
+    pieces, beside = lax.optimization_barrier((exchange(pieces), beside))
+    gate, res, out_t, in_t, next_out_t, up_t, down_t = beside
+    mixed = exchange(product(False, pieces))
+    pieces, res, gate = middle(mixed, mask, res, gate, out_t, in_t)
     mixed = exchange(product(True, exchange(pieces)))
-    return last(mixed, res, gate, inc_out_w, trans_up, trans_down)
+    return last(mixed, res, gate, next_out_t, up_t, down_t)
 
 
 def solution(mesh):

time: 102 us -> 99.7 us (0.977)
  waiting for transfers between devices: 26.3 us -> 11.5 us
  local copies, waits for them, and re-layouts: 0.05 us -> 7.42 us
  starting transfers between devices: 7.37 us -> 11.5 us
  blocking collectives: 54.4 us -> 57.9 us
  Pallas kernels: 13.3 us -> 10.7 us
    all_to_all x2 -> x1, waiting for transfers between devices: 26.3 us -> 11.5 us  [exchange(): return lax.all_to_all(x, ('row', 'col'), 0, 0, tiled=True)]
    unnamed x18 -> x34, local copies, waits for them, and re-layouts: 0.05 us -> 7.42 us
    all_to_all x2 -> x1, starting transfers between devices: 7.37 us -> 11.5 us  [exchange(): return lax.all_to_all(x, ('row', 'col'), 0, 0, tiled=True)]
    all_to_all x2 -> x3, blocking collectives: 54.4 us -> 57.9 us  [exchange(): return lax.all_to_all(x, ('row', 'col'), 0, 0, tiled=True)]
    pallas_call x6 -> x5, Pallas kernels: 10.2 us -> 7.61 us  [local(): pl.pallas_call(kernel, out_shape=out, in_specs=[VMEM] * len(args), out_sp...]
  transfers between devices with their start and end apart: 2 -> 1, of which waited for: 2 -> 1; matrix products, arithmetic and copies ran while one was open for 0% -> 0% of each run, Pallas kernels for 1% -> 1%
where the time goes in v3:
time: 99.7 us; the launch traced here: 99.1 us
  blocking collectives  57.9 us (58%)
  starting transfers between devices  11.5 us (12%)
  waiting for transfers between devices  11.5 us (12%)
  Pallas kernels  10.7 us (11%)
  local copies, waits for them, and re-layouts  7.42 us (7%)
    all_to_all x3, blocking collectives, exchange(): return lax.all_to_all(x, ('row', 'col'), 0, 0, tiled=True)  57.9 us
    all_to_all x1, starting transfers between devices, exchange(): return lax.all_to_all(x, ('row', 'col'), 0, 0, tiled=True)  11.5 us
    all_to_all x1, waiting for transfers between devices, exchange(): return lax.all_to_all(x, ('row', 'col'), 0, 0, tiled=True)  11.5 us
    pallas_call x5, Pallas kernels, local(): pl.pallas_call(kernel, out_shape=out, in_specs=[VMEM] * len(args), out_sp...  7.61 us
    unnamed x34, local copies, waits for them, and re-layouts  7.42 us
    pallas_call x1, Pallas kernels, first(): pl.pallas_call(first_kernel, out_shape=(PIECES, MASK), in_specs=[ANY] * 3...  3.07 us
  transfers between devices with their start and end apart: 1, of which 1 were waited for; matrix products, arithmetic and copies ran while one was open for 0% of the time, Pallas kernels for 1%

profile of v3, /device:TPU:1, one launch (start us, length us, event | category | flops | bytes accessed | tf_op | source)
XLA Modules:
  0.0 99.1 jit_solution(8007975999451309448)
XLA Ops:
  0.0 3.1 %shard_map.100 = (bf16[128,32,128]{2,1,0:T(8,128)(2,1)}, f32[16,128]{1,0:T(8,128)}) custom-call(bf16[32,64,128]{2,1,0:T(8,128)(2,1)} %pair_ref, bf16[128,512]{1,0:T(8,128)(2,1)} %w_in_hbm.1, s32[4,128]{1,0:T(4,128)} %bitcast.9), custom_call_target="tpu_custom_call" | custom-call | tf_op jit(solution)/shard_map/pallas_call | solution.py:214
  3.1 0.0 copy-start
  3.1 0.0 copy-start.4
  3.1 11.5 %all-to-all-start = ((bf16[128,32,128]{2,1,0:T(8,128)(2,1)}), bf16[128,32,128]{2,1,0:T(8,128)(2,1)S(1)}, u32[]{:S(2)}, u32[]{:S(2)}) async-start(bf16[128,32,128]{2,1,0:T(8,128)(2,1)} %get-tuple-element.28), calls=%async_computation | async-start | bytes 2097152 | tf_op jit(solution)/shard_map/all_to_all | solution.py:255
  14.6 0.0 copy-done
  14.6 0.0 copy-done.4
  14.6 0.0 copy-start.1
  14.6 0.9 copy-done.1
  15.6 0.9 copy-done.5
  16.5 0.8 copy-done.12
  17.3 0.8 copy-done.13
  18.0 0.8 copy-done.14
  18.8 0.8 copy-done.15
  19.5 0.7 shard_map.101
  20.2 0.0 copy-start.2
  20.2 0.7 copy-done.2
  20.9 0.6 copy-done.6
  21.5 0.6 copy-done.8
  22.1 0.6 copy-done.10
  22.7 11.5 %all-to-all-done = bf16[128,32,128]{2,1,0:T(8,128)(2,1)S(1)} async-done(((bf16[128,32,128]{2,1,0:T(8,128)(2,1)}), bf16[128,32,128]{2,1,0:T(8,128)(2,1)S(1)}, u32[]{:S(2)}, u32[]{:S(2)}) %all-to-all-start) | async-done | bytes 1048608 | tf_op jit(solution)/shard_map/all_to_all | solution.py:255
  34.2 0.7 shard_map.102
  34.9 0.0 copy-start.3
  34.9 0.0 copy-start.11
  34.9 0.0 copy-start.16
  35.0 17.3 %all_to_all.20.mixed_ref = bf16[128,16,128]{2,1,0:T(8,128)(2,1)S(1)} all-to-all(bf16[128,16,128]{2,1,0:T(8,128)(2,1)S(1)} %bitcast.7), channel_id=1, replica_groups=mesh['row'=16,'col'=8] {'row','col'}, dimensions={0} | all-to-all | bytes 1048576 | tf_op jit(solution)/shard_map/all_to_all | solution.py:255
  52.3 0.0 copy-done.16
  52.3 2.1 %shard_map.103 = (bf16[128,32,128]{2,1,0:T(8,128)(2,1)S(1)}, bf16[128,2048]{1,0:T(8,128)(2,1)S(1)}, f32[128,2048]{1,0:T(8,128)S(1)}) custom-call(bf16[128,16,128]{2,1,0:T(8,128)(2,1)S(1)} %all_to_all.20.mixed_ref, f32[16,128]{1,0:T(8,128)S(1)} %copy-done.16, bf16[128,2048]{1,0:T(8,128)(2,1)S(1)} %get-tuple-element.39.res_ref, ...), custom_call_target="tpu_custom_call" | custom-call | tf_op jit(solution)/shard_map/pallas_call | solution.py:202
  54.4 23.3 %all_to_all.21 = bf16[128,32,128]{2,1,0:T(8,128)(2,1)S(1)} all-to-all(bf16[128,32,128]{2,1,0:T(8,128)(2,1)S(1)} %get-tuple-element.43), channel_id=1, replica_groups=mesh['row'=16,'col'=8] {'row','col'}, dimensions={0} | all-to-all | bytes 2097152 | tf_op jit(solution)/shard_map/all_to_all | solution.py:255
  77.7 1.1 %shard_map.104 = bf16[16,8,16,128]{3,2,1,0:T(8,128)(2,1)S(1)} custom-call(bf16[16,8,32,128]{3,2,1,0:T(8,128)(2,1)S(1)} %bitcast.6), custom_call_target="tpu_custom_call" | custom-call | tf_op jit(solution)/shard_map/pallas_call | solution.py:202
  78.7 17.3 %all_to_all.22.mixed_ref = bf16[128,16,128]{2,1,0:T(8,128)(2,1)S(1)} all-to-all(bf16[128,16,128]{2,1,0:T(8,128)(2,1)S(1)} %bitcast.8), channel_id=1, replica_groups=mesh['row'=16,'col'=8] {'row','col'}, dimensions={0} | all-to-all | bytes 1048576 | tf_op jit(solution)/shard_map/all_to_all | solution.py:255
  96.0 0.0 copy-done.9
  96.0 3.1 %shard_map.105 = bf16[32,64,128]{2,1,0:T(8,128)(2,1)} custom-call(bf16[128,16,128]{2,1,0:T(8,128)(2,1)S(1)} %all_to_all.22.mixed_ref, bf16[128,2048]{1,0:T(8,128)(2,1)S(1)} %get-tuple-element.44.res_ref, f32[128,2048]{1,0:T(8,128)S(1)} %get-tuple-element.45.gate_ref, bf16[128,128]{1,0:T(8,128)(2,1)S(1)} %copy-done.9, ...), custom_call_target="tpu_custom_call" | custom-call | tf_op jit(solution)/shard_map/pallas_call | solution.py:202
  (13 shorter events, 0.0 us)
Async XLA Ops:
  3.1 11.5 %copy-start = (bf16[32,64,128]{2,1,0:T(8,128)(2,1)S(1)}, bf16[32,64,128]{2,1,0:T(8,128)(2,1)}, u32[]{:S(2)}) copy-start(bf16[32,64,128]{2,1,0:T(8,128)(2,1)} %pair_ref) | copy-start | bytes 1572868
  3.1 11.5 %copy-start.4 = (bf16[128,512]{1,0:T(8,128)(2,1)S(1)}, bf16[128,512]{1,0:T(8,128)(2,1)}, u32[]{:S(2)}) copy-start(bf16[128,512]{1,0:T(8,128)(2,1)} %in_w_ref.1) | copy-start | bytes 393220
  3.1 31.1 %all-to-all-start = ((bf16[128,32,128]{2,1,0:T(8,128)(2,1)}), bf16[128,32,128]{2,1,0:T(8,128)(2,1)S(1)}, u32[]{:S(2)}, u32[]{:S(2)}) async-start(bf16[128,32,128]{2,1,0:T(8,128)(2,1)} %get-tuple-element.28), calls=%async_computation | async-start | bytes 2097152 | tf_op jit(solution)/shard_map/all_to_all | solution.py:255
  14.6 1.0 copy-start.1
  15.6 0.9 copy-start.5
  16.5 0.8 copy-start.12
  17.3 0.8 copy-start.13
  18.0 0.8 copy-start.14
  18.8 0.8 copy-start.15
  20.2 0.7 copy-start.2
  20.9 0.7 copy-start.6
  21.5 0.6 copy-start.8
  22.1 0.6 copy-start.10
  34.9 17.3 %copy-start.3 = (bf16[640,128]{1,0:T(8,128)(2,1)S(1)}, bf16[640,128]{1,0:T(8,128)(2,1)}, u32[]{:S(2)}) copy-start(bf16[640,128]{1,0:T(8,128)(2,1)} %copy-done.2) | copy-start | bytes 491524
  34.9 17.3 %copy-start.11 = (bf16[128,128]{1,0:T(8,128)(2,1)S(1)}, bf16[128,128]{1,0:T(8,128)(2,1)}, u32[]{:S(2)}) copy-start(bf16[128,128]{1,0:T(8,128)(2,1)} %copy-done.10) | copy-start | bytes 98308
  34.9 17.3 %copy-start.16 = (f32[16,128]{1,0:T(8,128)S(1)}, f32[16,128]{1,0:T(8,128)}, u32[]{:S(2)}) copy-start(f32[16,128]{1,0:T(8,128)} %get-tuple-element.38.mask_ref) | copy-start | bytes 24580
  78.7 17.3 %copy-start.7 = (bf16[128,512]{1,0:T(8,128)(2,1)S(1)}, bf16[128,512]{1,0:T(8,128)(2,1)}, u32[]{:S(2)}) copy-start(bf16[128,512]{1,0:T(8,128)(2,1)} %copy-done.6) | copy-start | bytes 393220
  78.7 17.3 %copy-start.9 = (bf16[128,128]{1,0:T(8,128)(2,1)S(1)}, bf16[128,128]{1,0:T(8,128)(2,1)}, u32[]{:S(2)}) copy-start(bf16[128,128]{1,0:T(8,128)(2,1)} %copy-done.8) | copy-start | bytes 98308

commit v4 on v3

--- a/solution.py
+++ b/solution.py
@@ -15,13 +15,7 @@
 SPOTS = ROWS * COLS
 DEVS = 128
 STAGE = 40
-SCALED = 24
-
-
-def tree(parts):
-    while len(parts) > 1:
-        parts = [a + b for a, b in zip(parts[::2], parts[1::2])]
-    return parts[0]
+ROW_STEP = 24
 
 
 def normalize(x):
@@ -53,14 +47,13 @@
     return jnp.dot(w, normalize(x), preferred_element_type=F32)
 
 
-def stage_operands(p, mask_ref, s0, count, stage):
-    mask = jnp.concatenate([mask_ref[s0 + n : s0 + n + 1, :] for n in range(count)], axis=1)
-    half_mask = 0.5 * mask
+def stage_operands(p, mask_ref, stage):
+    half_mask = 0.5 * jnp.concatenate([mask_ref[s : s + 1, :] for s in range(HALF)], axis=1)
     for at, k in ((0, 0), (HALF, 256)):
         value = half_mask * p[k + 128 : k + 256]
         value = value * jnp.tanh(0.5 * p[k : k + 128]) + value
-        for n in range(count):
-            stage[pl.ds(at + s0 + n, DEVS, stride=STAGE), :] = value[:, n * LANES : (n + 1) * LANES]
+        for s in range(HALF):
+            stage[pl.ds(at + s, DEVS, stride=STAGE), :] = value[:, s * LANES : (s + 1) * LANES]
 
 
 def put_pieces(stage, pieces_ref):
@@ -86,9 +79,8 @@
         copy.wait()
     put_mask(present_ref, mask_ref)
     w = w_in_ref[...].T
-    for s in range(0, HALF, 8):
-        p = project(load_steps(pair_ref, s, 8).astype(F32), w)
-        stage_operands(p, mask_ref, s, 8, stage)
+    p = project(load_steps(pair_ref, 0, HALF).astype(F32), w)
+    stage_operands(p, mask_ref, stage)
     put_pieces(stage, pieces_ref)
 
 
@@ -135,55 +127,52 @@
         out_ref[:, 2 * pair + 1] = b.reshape(16, HALF, LANES)
 
 
-def scale_mixed(mixed_ref, scaled):
-    sums = [None] * 8
+def unpack(mixed_ref, rows):
     for h in range(DEVS):
-        value = mixed_ref[h].astype(F32)
-        sums[h % 8] = value if h < 8 else sums[h % 8] + value
-    mean = tree(sums) * (1.0 / 128)
-    for h in range(DEVS):
-        center = mixed_ref[h].astype(F32) - mean
-        sums[h % 8] = center * center if h < 8 else sums[h % 8] + center * center
-    factor = lax.rsqrt(jnp.maximum(tree(sums) * (1.0 / 128), 1.0))
-    for h in range(DEVS):
-        scaled[h * SCALED : h * SCALED + HALF, :] = (mixed_ref[h].astype(F32) - mean) * factor
-
-
-def finish(scaled, s0, count, w_out, res_ref, gate_ref):
+        rows[h * ROW_STEP : h * ROW_STEP + HALF, :] = mixed_ref[h].astype(F32)
+
+
+def scaled_step(rows, s):
+    value = rows[pl.ds(s, DEVS, stride=ROW_STEP), :]
+    center = value - jnp.mean(value, axis=0, keepdims=True)
+    spread = jnp.mean(center * center, axis=0, keepdims=True)
+    return (center * lax.rsqrt(jnp.maximum(spread, 1.0))).astype(BF16)
+
+
+def finish(rows, s0, count, w_out, res_ref, gate_ref):
     lanes = slice(s0 * LANES, (s0 + count) * LANES)
-    rows = [
-        scaled[pl.ds(s0 + n, DEVS, stride=SCALED), :].astype(BF16) for n in range(count)
-    ]
-    update = jnp.dot(w_out, jnp.concatenate(rows, axis=1), preferred_element_type=F32)
+    scaled = jnp.concatenate([scaled_step(rows, s0 + n) for n in range(count)], axis=1)
+    update = jnp.dot(w_out, scaled, preferred_element_type=F32)
     return (res_ref[:, lanes].astype(F32) + gate_ref[:, lanes] * update).astype(BF16)
 
 
 def middle_kernel(
     mixed_ref, mask_ref, res_ref, gate_ref, w_out_ref, w_in_ref,
-    pieces_ref, first_ref, next_gate_ref, scaled, stage,
-):
-    scale_mixed(mixed_ref, scaled)
-    for s in range(0, HALF, 8):
-        lanes = slice(s * LANES, (s + 8) * LANES)
-        x = finish(scaled, s, 8, w_out_ref[...], res_ref, gate_ref)
-        first_ref[:, lanes] = x
-        p = project(x.astype(F32), w_in_ref[...])
-        stage_operands(p, mask_ref, s, 8, stage)
-        next_gate_ref[:, lanes] = sigmoid(p[512:])
+    pieces_ref, first_ref, next_gate_ref, rows, stage,
+):
+    unpack(mixed_ref, rows)
+    x = finish(rows, 0, HALF, w_out_ref[...], res_ref, gate_ref)
+    first_ref[...] = x
+    p = project(x.astype(F32), w_in_ref[...])
+    stage_operands(p, mask_ref, stage)
+    next_gate_ref[...] = sigmoid(p[512:])
     put_pieces(stage, pieces_ref)
 
 
-def last_kernel(mixed_ref, res_ref, gate_ref, w_out_ref, up_ref, down_ref, out_ref, scaled):
-    scale_mixed(mixed_ref, scaled)
-    x = finish(scaled, 0, HALF, w_out_ref[...], res_ref, gate_ref).astype(F32)
-    p = project(x, up_ref[...])
-    half = (0.5 * p[:512]).astype(BF16)
-    hidden = (half * jnp.tanh(half) + half) * p[512:].astype(BF16)
-    y = x + jnp.dot(down_ref[...], hidden, preferred_element_type=F32)
-    y = y.astype(BF16).T
-    for s in range(HALF):
-        out_ref[s] = y[2 * s * COLS : (2 * s + 1) * COLS]
-        out_ref[HALF + s] = y[(2 * s + 1) * COLS : (2 * s + 2) * COLS]
+def last_kernel(mixed_ref, res_ref, gate_ref, w_out_ref, up_ref, down_ref, out_ref, rows):
+    unpack(mixed_ref, rows)
+    starts = range(0, HALF, 8)
+    tiles = [finish(rows, s, 8, w_out_ref[...], res_ref, gate_ref) for s in starts]
+    for s, x in zip(starts, tiles):
+        x = x.astype(F32)
+        p = project(x, up_ref[...])
+        half = (0.5 * p[:512]).astype(BF16)
+        hidden = (half * jnp.tanh(half) + half) * p[512:].astype(BF16)
+        y = x + jnp.dot(down_ref[...], hidden, preferred_element_type=F32)
+        y = y.astype(BF16).T
+        for n in range(8):
+            out_ref[s + n] = y[2 * n * COLS : (2 * n + 1) * COLS]
+            out_ref[HALF + s + n] = y[(2 * n + 1) * COLS : (2 * n + 2) * COLS]
 
 
 VMEM = pl.BlockSpec(memory_space=pltpu.VMEM)
@@ -194,8 +183,8 @@
 GATE = jax.ShapeDtypeStruct((CHANS, SPOTS), F32)
 RES = jax.ShapeDtypeStruct((CHANS, SPOTS), BF16)
 TILE = jax.ShapeDtypeStruct((ROWS, COLS, CHANS), BF16)
-STAGE_T = pltpu.VMEM((DEVS * STAGE, LANES), F32)
-SCALED_T = pltpu.VMEM((DEVS * SCALED, LANES), F32)
+STAGE_T = pltpu.VMEM(((DEVS + 1) * STAGE, LANES), F32)
+ROWS_T = pltpu.VMEM(((DEVS + 1) * ROW_STEP, LANES), F32)
 
 
 def local(kernel, out, scratch, args, limit=32, flops=0, moved=0):
@@ -244,11 +233,11 @@
 
 
 def middle(*args):
-    return local(middle_kernel, (PIECES, RES, GATE), [SCALED_T, STAGE_T], args)
+    return local(middle_kernel, (PIECES, RES, GATE), [ROWS_T, STAGE_T], args)
 
 
 def last(*args):
-    return local(last_kernel, TILE, [SCALED_T], args)
+    return local(last_kernel, TILE, [ROWS_T], args)
 
 
 def exchange(x):

time: 99.7 us -> 99.3 us (level)
  no operation moved by 1% of the time
where the time goes in v4:
time: 99.3 us; the launch traced here: 98.7 us
  blocking collectives  57.9 us (58%)
  starting transfers between devices  11.5 us (12%)
  waiting for transfers between devices  11.5 us (12%)
  Pallas kernels  10.3 us (10%)
  local copies, waits for them, and re-layouts  7.42 us (7%)
    all_to_all x3, blocking collectives, exchange(): return lax.all_to_all(x, ('row', 'col'), 0, 0, tiled=True)  57.9 us
    all_to_all x1, starting transfers between devices, exchange(): return lax.all_to_all(x, ('row', 'col'), 0, 0, tiled=True)  11.5 us
    all_to_all x1, waiting for transfers between devices, exchange(): return lax.all_to_all(x, ('row', 'col'), 0, 0, tiled=True)  11.5 us
    unnamed x34, local copies, waits for them, and re-layouts  7.42 us
    pallas_call x5, Pallas kernels, local(): pl.pallas_call(kernel, out_shape=out, in_specs=[VMEM] * len(args), out_sp...  7.22 us
    pallas_call x1, Pallas kernels, first(): pl.pallas_call(first_kernel, out_shape=(PIECES, MASK), in_specs=[ANY] * 3...  3.07 us
  transfers between devices with their start and end apart: 1, of which 1 were waited for; matrix products, arithmetic and copies ran while one was open for 0% of the time, Pallas kernels for 1%

profile of v4, /device:TPU:1, one launch (start us, length us, event | category | flops | bytes accessed | tf_op | source)
XLA Modules:
  0.0 98.7 jit_solution(7966150622475609465)
XLA Ops:
  0.0 3.1 %shard_map.100 = (bf16[128,32,128]{2,1,0:T(8,128)(2,1)}, f32[16,128]{1,0:T(8,128)}) custom-call(bf16[32,64,128]{2,1,0:T(8,128)(2,1)} %pair_ref, bf16[128,512]{1,0:T(8,128)(2,1)} %w_in_hbm.1, s32[4,128]{1,0:T(4,128)} %bitcast.9), custom_call_target="tpu_custom_call" | custom-call | tf_op jit(solution)/shard_map/pallas_call | solution.py:203
  3.1 0.0 copy-start
  3.1 0.0 copy-start.4
  3.1 11.5 %all-to-all-start = ((bf16[128,32,128]{2,1,0:T(8,128)(2,1)}), bf16[128,32,128]{2,1,0:T(8,128)(2,1)S(1)}, u32[]{:S(2)}, u32[]{:S(2)}) async-start(bf16[128,32,128]{2,1,0:T(8,128)(2,1)} %get-tuple-element.28), calls=%async_computation | async-start | bytes 2097152 | tf_op jit(solution)/shard_map/all_to_all | solution.py:244
  14.6 0.0 copy-done
  14.6 0.0 copy-done.4
  14.6 0.0 copy-start.1
  14.6 0.9 copy-done.1
  15.6 0.9 copy-done.5
  16.5 0.8 copy-done.12
  17.3 0.8 copy-done.13
  18.0 0.8 copy-done.14
  18.8 0.8 copy-done.15
  19.5 0.7 shard_map.101
  20.2 0.0 copy-start.2
  20.2 0.7 copy-done.2
  20.9 0.6 copy-done.6
  21.5 0.6 copy-done.8
  22.1 0.6 copy-done.10
  22.7 11.5 %all-to-all-done = bf16[128,32,128]{2,1,0:T(8,128)(2,1)S(1)} async-done(((bf16[128,32,128]{2,1,0:T(8,128)(2,1)}), bf16[128,32,128]{2,1,0:T(8,128)(2,1)S(1)}, u32[]{:S(2)}, u32[]{:S(2)}) %all-to-all-start) | async-done | bytes 1048608 | tf_op jit(solution)/shard_map/all_to_all | solution.py:244
  34.2 0.7 shard_map.102
  34.9 0.0 copy-start.3
  34.9 0.0 copy-start.11
  34.9 0.0 copy-start.16
  35.0 17.3 %all_to_all.20.mixed_ref = bf16[128,16,128]{2,1,0:T(8,128)(2,1)S(1)} all-to-all(bf16[128,16,128]{2,1,0:T(8,128)(2,1)S(1)} %bitcast.7), channel_id=1, replica_groups=mesh['row'=16,'col'=8] {'row','col'}, dimensions={0} | all-to-all | bytes 1048576 | tf_op jit(solution)/shard_map/all_to_all | solution.py:244
  52.2 0.0 copy-done.3
  52.3 1.7 %shard_map.103 = (bf16[128,32,128]{2,1,0:T(8,128)(2,1)S(1)}, bf16[128,2048]{1,0:T(8,128)(2,1)S(1)}, f32[128,2048]{1,0:T(8,128)S(1)}) custom-call(bf16[128,16,128]{2,1,0:T(8,128)(2,1)S(1)} %all_to_all.20.mixed_ref, f32[16,128]{1,0:T(8,128)S(1)} %copy-done.16, bf16[128,2048]{1,0:T(8,128)(2,1)S(1)} %get-tuple-element.39.res_ref, ...), custom_call_target="tpu_custom_call" | custom-call | tf_op jit(solution)/shard_map/pallas_call | solution.py:191
  54.0 23.3 %all_to_all.21 = bf16[128,32,128]{2,1,0:T(8,128)(2,1)S(1)} all-to-all(bf16[128,32,128]{2,1,0:T(8,128)(2,1)S(1)} %get-tuple-element.43), channel_id=1, replica_groups=mesh['row'=16,'col'=8] {'row','col'}, dimensions={0} | all-to-all | bytes 2097152 | tf_op jit(solution)/shard_map/all_to_all | solution.py:244
  77.3 1.1 %shard_map.104 = bf16[16,8,16,128]{3,2,1,0:T(8,128)(2,1)S(1)} custom-call(bf16[16,8,32,128]{3,2,1,0:T(8,128)(2,1)S(1)} %bitcast.6), custom_call_target="tpu_custom_call" | custom-call | tf_op jit(solution)/shard_map/pallas_call | solution.py:191
  78.4 17.3 %all_to_all.22.mixed_ref = bf16[128,16,128]{2,1,0:T(8,128)(2,1)S(1)} all-to-all(bf16[128,16,128]{2,1,0:T(8,128)(2,1)S(1)} %bitcast.8), channel_id=1, replica_groups=mesh['row'=16,'col'=8] {'row','col'}, dimensions={0} | all-to-all | bytes 1048576 | tf_op jit(solution)/shard_map/all_to_all | solution.py:244
  95.7 0.0 copy-done.9
  95.7 3.0 %shard_map.105 = bf16[32,64,128]{2,1,0:T(8,128)(2,1)} custom-call(bf16[128,16,128]{2,1,0:T(8,128)(2,1)S(1)} %all_to_all.22.mixed_ref, bf16[128,2048]{1,0:T(8,128)(2,1)S(1)} %get-tuple-element.44.res_ref, f32[128,2048]{1,0:T(8,128)S(1)} %get-tuple-element.45.gate_ref, bf16[128,128]{1,0:T(8,128)(2,1)S(1)} %copy-done.9, ...), custom_call_target="tpu_custom_call" | custom-call | tf_op jit(solution)/shard_map/pallas_call | solution.py:191
  (13 shorter events, 0.0 us)
Async XLA Ops:
  3.1 11.5 %copy-start = (bf16[32,64,128]{2,1,0:T(8,128)(2,1)S(1)}, bf16[32,64,128]{2,1,0:T(8,128)(2,1)}, u32[]{:S(2)}) copy-start(bf16[32,64,128]{2,1,0:T(8,128)(2,1)} %pair_ref) | copy-start | bytes 1572868
  3.1 11.5 %copy-start.4 = (bf16[128,512]{1,0:T(8,128)(2,1)S(1)}, bf16[128,512]{1,0:T(8,128)(2,1)}, u32[]{:S(2)}) copy-start(bf16[128,512]{1,0:T(8,128)(2,1)} %in_w_ref.1) | copy-start | bytes 393220
  3.1 31.1 %all-to-all-start = ((bf16[128,32,128]{2,1,0:T(8,128)(2,1)}), bf16[128,32,128]{2,1,0:T(8,128)(2,1)S(1)}, u32[]{:S(2)}, u32[]{:S(2)}) async-start(bf16[128,32,128]{2,1,0:T(8,128)(2,1)} %get-tuple-element.28), calls=%async_computation | async-start | bytes 2097152 | tf_op jit(solution)/shard_map/all_to_all | solution.py:244
  14.6 1.0 copy-start.1
  15.6 0.9 copy-start.5
  16.5 0.8 copy-start.12
  17.3 0.8 copy-start.13
  18.0 0.8 copy-start.14
  18.8 0.8 copy-start.15
  20.2 0.7 copy-start.2
  20.9 0.7 copy-start.6
  21.5 0.6 copy-start.8
  22.1 0.6 copy-start.10
  34.9 17.3 %copy-start.3 = (bf16[640,128]{1,0:T(8,128)(2,1)S(1)}, bf16[640,128]{1,0:T(8,128)(2,1)}, u32[]{:S(2)}) copy-start(bf16[640,128]{1,0:T(8,128)(2,1)} %copy-done.2) | copy-start | bytes 491524
  34.9 17.3 %copy-start.11 = (bf16[128,128]{1,0:T(8,128)(2,1)S(1)}, bf16[128,128]{1,0:T(8,128)(2,1)}, u32[]{:S(2)}) copy-start(bf16[128,128]{1,0:T(8,128)(2,1)} %copy-done.10) | copy-start | bytes 98308
  34.9 17.3 %copy-start.16 = (f32[16,128]{1,0:T(8,128)S(1)}, f32[16,128]{1,0:T(8,128)}, u32[]{:S(2)}) copy-start(f32[16,128]{1,0:T(8,128)} %get-tuple-element.38.mask_ref) | copy-start | bytes 24580
  78.4 17.3 %copy-start.7 = (bf16[128,512]{1,0:T(8,128)(2,1)S(1)}, bf16[128,512]{1,0:T(8,128)(2,1)}, u32[]{:S(2)}) copy-start(bf16[128,512]{1,0:T(8,128)(2,1)} %copy-done.6) | copy-start | bytes 393220
  78.4 17.3 %copy-start.9 = (bf16[128,128]{1,0:T(8,128)(2,1)S(1)}, bf16[128,128]{1,0:T(8,128)(2,1)}, u32[]{:S(2)}) copy-start(bf16[128,128]{1,0:T(8,128)(2,1)} %copy-done.8) | copy-start | bytes 98308

commit v5 on v4

--- a/solution.py
+++ b/solution.py
@@ -14,6 +14,19 @@
 LANES = 2 * COLS
 SPOTS = ROWS * COLS
 DEVS = 128
+NATURAL = tuple(range(DEVS))
+
+
+def far_first():
+    def place(device):
+        row, col = divmod(device, 8)
+        at = (row // 4, col % 2 * 2 + row // 2 % 2, col // 2)
+        return sum(min(k, 4 - k) for k in at), at, row % 2
+
+    return tuple(sorted(range(DEVS), key=place, reverse=True))
+
+
+FAR_FIRST = far_first()
 STAGE = 40
 ROW_STEP = 24
 
@@ -86,7 +99,7 @@
 
 def side_kernel(
     pair_ref, gate_w_ref, out_w_ref, in_w_ref, next_gate_w_ref, next_out_w_ref, up_ref, down_ref,
-    gate_ref, res_ref, out_t_ref, in_t_ref, next_out_t_ref, up_t_ref, down_t_ref,
+    gate_ref, res_ref, out_t_ref, in_t_ref, next_out_t_ref, up_t_ref, down_t_ref, channels, ordered,
 ):
     w = gate_w_ref[...].T
     for s in range(0, HALF, 8):
@@ -97,12 +110,15 @@
     out_t_ref[...] = out_w_ref[...].T
     in_t_ref[:512] = in_w_ref[...].T
     in_t_ref[512:] = next_gate_w_ref[...].T
-    next_out_t_ref[...] = next_out_w_ref[...].T
+    channels[...] = next_out_w_ref[...].astype(F32)
+    for n, channel in enumerate(FAR_FIRST):
+        ordered[n : n + 1, :] = channels[channel : channel + 1, :]
+    next_out_t_ref[...] = ordered[...].T.astype(BF16)
     up_t_ref[...] = up_ref[...].T
     down_t_ref[...] = down_ref[...].T
 
 
-def product_kernel(incoming, x_ref, out_ref, left, right):
+def product_kernel(incoming, order, x_ref, out_ref, left, right):
     for at, whole in ((0, left), (HALF, right)):
         for pair in range(4):
             a = x_ref[:, 2 * pair, at : at + HALF, :].reshape(16 * HALF, LANES)
@@ -123,8 +139,10 @@
         bottom = mixed[:, 1, :, lanes].reshape(16 * HALF, LANES)
         a = jnp.concatenate([top[:, :COLS], bottom[:, :COLS]], axis=1)
         b = jnp.concatenate([top[:, COLS:], bottom[:, COLS:]], axis=1)
-        out_ref[:, 2 * pair] = a.reshape(16, HALF, LANES)
-        out_ref[:, 2 * pair + 1] = b.reshape(16, HALF, LANES)
+        for row in range(16):
+            tile = slice(row * HALF, (row + 1) * HALF)
+            out_ref[order.index(row * 8 + 2 * pair)] = a[tile]
+            out_ref[order.index(row * 8 + 2 * pair + 1)] = b[tile]
 
 
 def unpack(mixed_ref, rows):
@@ -179,7 +197,7 @@
 ANY = pl.BlockSpec(memory_space=pl.ANY)
 PIECES = jax.ShapeDtypeStruct((DEVS, 2 * HALF, LANES), BF16)
 MASK = jax.ShapeDtypeStruct((HALF, LANES), F32)
-MIXED = jax.ShapeDtypeStruct((16, 8, HALF, LANES), BF16)
+MIXED = jax.ShapeDtypeStruct((DEVS, HALF, LANES), BF16)
 GATE = jax.ShapeDtypeStruct((CHANS, SPOTS), F32)
 RES = jax.ShapeDtypeStruct((CHANS, SPOTS), BF16)
 TILE = jax.ShapeDtypeStruct((ROWS, COLS, CHANS), BF16)
@@ -222,14 +240,14 @@
 
 def side(*args):
     out = (GATE, RES, weight(128), weight(640), weight(128), weight(1024), weight(128, 512))
-    return local(side_kernel, out, [], args, flops=1 << 28, moved=6 << 20)
-
-
-def product(incoming, pieces):
+    channels = pltpu.VMEM((DEVS, CHANS), F32)
+    return local(side_kernel, out, [channels, channels], args, flops=1 << 28, moved=6 << 20)
+
+
+def product(incoming, order, pieces):
     whole = pltpu.VMEM((16, 2, HALF, 512), BF16)
-    kernel = functools.partial(product_kernel, incoming)
-    mixed = local(kernel, MIXED, [whole, whole], (pieces.reshape(16, 8, 2 * HALF, LANES),))
-    return mixed.reshape(DEVS, HALF, LANES)
+    kernel = functools.partial(product_kernel, incoming, order)
+    return local(kernel, MIXED, [whole, whole], (pieces.reshape(16, 8, 2 * HALF, LANES),))
 
 
 def middle(*args):
@@ -240,8 +258,9 @@
     return local(last_kernel, TILE, [ROWS_T], args)
 
 
-def exchange(x):
-    return lax.all_to_all(x, ("row", "col"), 0, 0, tiled=True)
+def exchange(x, order=NATURAL):
+    groups = None if order == NATURAL else [list(order)]
+    return lax.all_to_all(x, ("row", "col"), 0, 0, axis_index_groups=groups, tiled=True)
 
 
 def on_device(
@@ -253,9 +272,9 @@
     beside = side(pair, out_gate_w, out_out_w, inc_in_w, inc_gate_w, inc_out_w, trans_up, trans_down)
     pieces, beside = lax.optimization_barrier((exchange(pieces), beside))
     gate, res, out_t, in_t, next_out_t, up_t, down_t = beside
-    mixed = exchange(product(False, pieces))
+    mixed = exchange(product(False, NATURAL, pieces))
     pieces, res, gate = middle(mixed, mask, res, gate, out_t, in_t)
-    mixed = exchange(product(True, exchange(pieces)))
+    mixed = exchange(product(True, FAR_FIRST, exchange(pieces)), FAR_FIRST)
     return last(mixed, res, gate, next_out_t, up_t, down_t)
 
 

time: 99.3 us -> 98.1 us (0.988)
  blocking collectives: 57.9 us -> 56.7 us
    all_to_all x3, blocking collectives: 57.9 us -> 56.7 us  [exchange(): lax.all_to_all(x, ('row', 'col'), 0, 0, axis_index_groups=groups, tiled=T...]
where the time goes in v5:
time: 98.1 us; the launch traced here: 97.6 us
  blocking collectives  56.7 us (58%)
  starting transfers between devices  11.5 us (12%)
  waiting for transfers between devices  11.5 us (12%)
  Pallas kernels  10.3 us (10%)
  local copies, waits for them, and re-layouts  7.42 us (8%)
    all_to_all x3, blocking collectives, exchange(): lax.all_to_all(x, ('row', 'col'), 0, 0, axis_index_groups=groups, tiled=T...  56.7 us
    all_to_all x1, starting transfers between devices, exchange(): lax.all_to_all(x, ('row', 'col'), 0, 0, axis_index_groups=groups, tiled=T...  11.5 us
    all_to_all x1, waiting for transfers between devices, exchange(): lax.all_to_all(x, ('row', 'col'), 0, 0, axis_index_groups=groups, tiled=T...  11.5 us
    unnamed x34, local copies, waits for them, and re-layouts  7.42 us
    pallas_call x5, Pallas kernels, local(): pl.pallas_call(kernel, out_shape=out, in_specs=[VMEM] * len(args), out_sp...  7.24 us
    pallas_call x1, Pallas kernels, first(): pl.pallas_call(first_kernel, out_shape=(PIECES, MASK), in_specs=[ANY] * 3...  3.07 us
  transfers between devices with their start and end apart: 1, of which 1 were waited for; matrix products, arithmetic and copies ran while one was open for 0% of the time, Pallas kernels for 1%

profile of v5, /device:TPU:1, one launch (start us, length us, event | category | flops | bytes accessed | tf_op | source)
XLA Modules:
  0.0 97.6 jit_solution(1665733291676784587)
XLA Ops:
  0.0 3.1 %shard_map.100 = (bf16[128,32,128]{2,1,0:T(8,128)(2,1)}, f32[16,128]{1,0:T(8,128)}) custom-call(bf16[32,64,128]{2,1,0:T(8,128)(2,1)} %pair_ref, bf16[128,512]{1,0:T(8,128)(2,1)} %w_in_hbm.1, s32[4,128]{1,0:T(4,128)} %bitcast.5), custom_call_target="tpu_custom_call" | custom-call | tf_op jit(solution)/shard_map/pallas_call | solution.py:221
  3.1 0.0 copy-start
  3.1 0.0 copy-start.4
  3.1 11.5 %all-to-all-start = ((bf16[128,32,128]{2,1,0:T(8,128)(2,1)}), bf16[128,32,128]{2,1,0:T(8,128)(2,1)S(1)}, u32[]{:S(2)}, u32[]{:S(2)}) async-start(bf16[128,32,128]{2,1,0:T(8,128)(2,1)} %get-tuple-element.28), calls=%async_computation | async-start | bytes 2097152 | tf_op jit(solution)/shard_map/all_to_all | solution.py:263
  14.6 0.0 copy-done
  14.6 0.0 copy-done.4
  14.6 0.0 copy-start.1
  14.6 0.9 copy-done.1
  15.6 0.9 copy-done.5
  16.5 0.8 copy-done.12
  17.3 0.8 copy-done.13
  18.0 0.8 copy-done.14
  18.8 0.8 copy-done.15
  19.5 0.7 shard_map.101
  20.2 0.0 copy-start.2
  20.2 0.7 copy-done.2
  20.9 0.6 copy-done.6
  21.5 0.6 copy-done.8
  22.1 0.6 copy-done.10
  22.7 11.5 %all-to-all-done = bf16[128,32,128]{2,1,0:T(8,128)(2,1)S(1)} async-done(((bf16[128,32,128]{2,1,0:T(8,128)(2,1)}), bf16[128,32,128]{2,1,0:T(8,128)(2,1)S(1)}, u32[]{:S(2)}, u32[]{:S(2)}) %all-to-all-start) | async-done | bytes 1048608 | tf_op jit(solution)/shard_map/all_to_all | solution.py:263
  34.2 0.7 shard_map.102
  34.9 0.0 copy-start.3
  34.9 0.0 copy-start.11
  34.9 0.0 copy-start.16
  35.0 17.3 %all_to_all.20.mixed_ref = bf16[128,16,128]{2,1,0:T(8,128)(2,1)S(1)} all-to-all(bf16[128,16,128]{2,1,0:T(8,128)(2,1)S(1)} %shard_map.102), channel_id=1, replica_groups=mesh['row'=16,'col'=8] {'row','col'}, dimensions={0} | all-to-all | bytes 1048576 | tf_op jit(solution)/shard_map/all_to_all | solution.py:263
  52.3 0.0 copy-done.16
  52.3 1.7 %shard_map.103 = (bf16[128,32,128]{2,1,0:T(8,128)(2,1)S(1)}, bf16[128,2048]{1,0:T(8,128)(2,1)S(1)}, f32[128,2048]{1,0:T(8,128)S(1)}) custom-call(bf16[128,16,128]{2,1,0:T(8,128)(2,1)S(1)} %all_to_all.20.mixed_ref, f32[16,128]{1,0:T(8,128)S(1)} %copy-done.16, bf16[128,2048]{1,0:T(8,128)(2,1)S(1)} %get-tuple-element.39.res_ref, ...), custom_call_target="tpu_custom_call" | custom-call | tf_op jit(solution)/shard_map/pallas_call | solution.py:209
  54.0 23.3 %all_to_all.21 = bf16[128,32,128]{2,1,0:T(8,128)(2,1)S(1)} all-to-all(bf16[128,32,128]{2,1,0:T(8,128)(2,1)S(1)} %get-tuple-element.43), channel_id=1, replica_groups=mesh['row'=16,'col'=8] {'row','col'}, dimensions={0} | all-to-all | bytes 2097152 | tf_op jit(solution)/shard_map/all_to_all | solution.py:263
  77.3 1.1 %shard_map.104 = bf16[128,16,128]{2,1,0:T(8,128)(2,1)S(1)} custom-call(bf16[16,8,32,128]{3,2,1,0:T(8,128)(2,1)S(1)} %bitcast.4), custom_call_target="tpu_custom_call" | custom-call | tf_op jit(solution)/shard_map/pallas_call | solution.py:209
  78.4 16.1 %all_to_all.22.mixed_ref = bf16[128,16,128]{2,1,0:T(8,128)(2,1)S(1)} all-to-all(bf16[128,16,128]{2,1,0:T(8,128)(2,1)S(1)} %shard_map.104), channel_id=1, replica_groups={{77,69,109,101,93,85,79,71,75,67,92,84,45,37,125,117,111,103,107,99,124..., dimensions={0} | all-to-all | bytes 1048576 | tf_op jit(solution)/shard_map/all_to_all | solution.py:263
  94.5 0.0 copy-done.7
  94.5 3.0 %shard_map.105 = bf16[32,64,128]{2,1,0:T(8,128)(2,1)} custom-call(bf16[128,16,128]{2,1,0:T(8,128)(2,1)S(1)} %all_to_all.22.mixed_ref, bf16[128,2048]{1,0:T(8,128)(2,1)S(1)} %get-tuple-element.44.res_ref, f32[128,2048]{1,0:T(8,128)S(1)} %get-tuple-element.45.gate_ref, bf16[128,128]{1,0:T(8,128)(2,1)S(1)} %copy-done.9, ...), custom_call_target="tpu_custom_call" | custom-call | tf_op jit(solution)/shard_map/pallas_call | solution.py:209
  (13 shorter events, 0.0 us)
Async XLA Ops:
  3.1 11.5 %copy-start = (bf16[32,64,128]{2,1,0:T(8,128)(2,1)S(1)}, bf16[32,64,128]{2,1,0:T(8,128)(2,1)}, u32[]{:S(2)}) copy-start(bf16[32,64,128]{2,1,0:T(8,128)(2,1)} %pair_ref) | copy-start | bytes 1572868
  3.1 11.5 %copy-start.4 = (bf16[128,512]{1,0:T(8,128)(2,1)S(1)}, bf16[128,512]{1,0:T(8,128)(2,1)}, u32[]{:S(2)}) copy-start(bf16[128,512]{1,0:T(8,128)(2,1)} %in_w_ref.1) | copy-start | bytes 393220
  3.1 31.1 %all-to-all-start = ((bf16[128,32,128]{2,1,0:T(8,128)(2,1)}), bf16[128,32,128]{2,1,0:T(8,128)(2,1)S(1)}, u32[]{:S(2)}, u32[]{:S(2)}) async-start(bf16[128,32,128]{2,1,0:T(8,128)(2,1)} %get-tuple-element.28), calls=%async_computation | async-start | bytes 2097152 | tf_op jit(solution)/shard_map/all_to_all | solution.py:263
  14.6 1.0 copy-start.1
  15.6 0.9 copy-start.5
  16.5 0.8 copy-start.12
  17.3 0.8 copy-start.13
  18.0 0.8 copy-start.14
  18.8 0.8 copy-start.15
  20.2 0.7 copy-start.2
  20.9 0.7 copy-start.6
  21.5 0.6 copy-start.8
  22.1 0.6 copy-start.10
  34.9 17.3 %copy-start.3 = (bf16[640,128]{1,0:T(8,128)(2,1)S(1)}, bf16[640,128]{1,0:T(8,128)(2,1)}, u32[]{:S(2)}) copy-start(bf16[640,128]{1,0:T(8,128)(2,1)} %copy-done.2) | copy-start | bytes 491524
  34.9 17.3 %copy-start.11 = (bf16[128,128]{1,0:T(8,128)(2,1)S(1)}, bf16[128,128]{1,0:T(8,128)(2,1)}, u32[]{:S(2)}) copy-start(bf16[128,128]{1,0:T(8,128)(2,1)} %copy-done.10) | copy-start | bytes 98308
  34.9 17.3 %copy-start.16 = (f32[16,128]{1,0:T(8,128)S(1)}, f32[16,128]{1,0:T(8,128)}, u32[]{:S(2)}) copy-start(f32[16,128]{1,0:T(8,128)} %get-tuple-element.38.mask_ref) | copy-start | bytes 24580
  78.4 16.2 %copy-start.7 = (bf16[128,512]{1,0:T(8,128)(2,1)S(1)}, bf16[128,512]{1,0:T(8,128)(2,1)}, u32[]{:S(2)}) copy-start(bf16[128,512]{1,0:T(8,128)(2,1)} %copy-done.6) | copy-start | bytes 393220
  78.4 16.2 %copy-start.9 = (bf16[128,128]{1,0:T(8,128)(2,1)S(1)}, bf16[128,128]{1,0:T(8,128)(2,1)}, u32[]{:S(2)}) copy-start(bf16[128,128]{1,0:T(8,128)(2,1)} %copy-done.8) | copy-start | bytes 98308

commit v6 on v5

--- a/solution.py
+++ b/solution.py
@@ -60,13 +60,14 @@
     return jnp.dot(w, normalize(x), preferred_element_type=F32)
 
 
-def stage_operands(p, mask_ref, stage):
-    half_mask = 0.5 * jnp.concatenate([mask_ref[s : s + 1, :] for s in range(HALF)], axis=1)
+def stage_operands(p, mask_ref, stage, s0=0):
+    steps = range(s0, s0 + p.shape[1] // LANES)
+    half_mask = 0.5 * jnp.concatenate([mask_ref[s : s + 1, :] for s in steps], axis=1)
     for at, k in ((0, 0), (HALF, 256)):
         value = half_mask * p[k + 128 : k + 256]
         value = value * jnp.tanh(0.5 * p[k : k + 128]) + value
-        for s in range(HALF):
-            stage[pl.ds(at + s, DEVS, stride=STAGE), :] = value[:, s * LANES : (s + 1) * LANES]
+        for n, s in enumerate(steps):
+            stage[pl.ds(at + s, DEVS, stride=STAGE), :] = value[:, n * LANES : (n + 1) * LANES]
 
 
 def put_pieces(stage, pieces_ref):
@@ -130,7 +131,9 @@
             whole[:, 1, :, lanes] = bottom.reshape(16, HALF, LANES)
     lhs = left[...].reshape(512, 512)
     rhs = right[...].reshape(512, 512)
-    dims = (((0,), (0,)), ((), ())) if incoming else (((1,), (1,)), ((), ()))
+    if incoming:
+        lhs = lhs.astype(F32).T.astype(BF16)
+    dims = (((1,), (0 if incoming else 1,)), ((), ()))
     mixed = lax.dot_general(lhs, rhs, dims, preferred_element_type=F32).astype(BF16)
     mixed = mixed.reshape(16, 2, HALF, 512)
     for pair in range(4):
@@ -169,11 +172,14 @@
     pieces_ref, first_ref, next_gate_ref, rows, stage,
 ):
     unpack(mixed_ref, rows)
-    x = finish(rows, 0, HALF, w_out_ref[...], res_ref, gate_ref)
-    first_ref[...] = x
-    p = project(x.astype(F32), w_in_ref[...])
-    stage_operands(p, mask_ref, stage)
-    next_gate_ref[...] = sigmoid(p[512:])
+    starts = range(0, HALF, 8)
+    tiles = [finish(rows, s, 8, w_out_ref[...], res_ref, gate_ref) for s in starts]
+    for s, x in zip(starts, tiles):
+        lanes = slice(s * LANES, (s + 8) * LANES)
+        first_ref[:, lanes] = x
+        p = project(x.astype(F32), w_in_ref[...])
+        stage_operands(p, mask_ref, stage, s)
+        next_gate_ref[:, lanes] = sigmoid(p[512:])
     put_pieces(stage, pieces_ref)
 
 

time: 98.1 us -> 98 us (level)
  no operation moved by 1% of the time
where the time goes in v6:
time: 98 us; the launch traced here: 97.4 us
  blocking collectives  56.7 us (58%)
  starting transfers between devices  11.5 us (12%)
  waiting for transfers between devices  11.5 us (12%)
  Pallas kernels  10.2 us (10%)
  local copies, waits for them, and re-layouts  7.42 us (8%)
    all_to_all x3, blocking collectives, exchange(): lax.all_to_all(x, ('row', 'col'), 0, 0, axis_index_groups=groups, tiled=T...  56.7 us
    all_to_all x1, starting transfers between devices, exchange(): lax.all_to_all(x, ('row', 'col'), 0, 0, axis_index_groups=groups, tiled=T...  11.5 us
    all_to_all x1, waiting for transfers between devices, exchange(): lax.all_to_all(x, ('row', 'col'), 0, 0, axis_index_groups=groups, tiled=T...  11.5 us
    unnamed x34, local copies, waits for them, and re-layouts  7.42 us
    pallas_call x5, Pallas kernels, local(): pl.pallas_call(kernel, out_shape=out, in_specs=[VMEM] * len(args), out_sp...  7.08 us
    pallas_call x1, Pallas kernels, first(): pl.pallas_call(first_kernel, out_shape=(PIECES, MASK), in_specs=[ANY] * 3...  3.07 us
  transfers between devices with their start and end apart: 1, of which 1 were waited for; matrix products, arithmetic and copies ran while one was open for 0% of the time, Pallas kernels for 1%

profile of v6, /device:TPU:1, one launch (start us, length us, event | category | flops | bytes accessed | tf_op | source)
XLA Modules:
  0.0 97.4 jit_solution(13911158827113388841)
XLA Ops:
  0.0 3.1 %shard_map.100 = (bf16[128,32,128]{2,1,0:T(8,128)(2,1)}, f32[16,128]{1,0:T(8,128)}) custom-call(bf16[32,64,128]{2,1,0:T(8,128)(2,1)} %pair_ref, bf16[128,512]{1,0:T(8,128)(2,1)} %w_in_hbm.1, s32[4,128]{1,0:T(4,128)} %bitcast.5), custom_call_target="tpu_custom_call" | custom-call | tf_op jit(solution)/shard_map/pallas_call | solution.py:227
  3.1 0.0 copy-start
  3.1 0.0 copy-start.4
  3.1 11.5 %all-to-all-start = ((bf16[128,32,128]{2,1,0:T(8,128)(2,1)}), bf16[128,32,128]{2,1,0:T(8,128)(2,1)S(1)}, u32[]{:S(2)}, u32[]{:S(2)}) async-start(bf16[128,32,128]{2,1,0:T(8,128)(2,1)} %get-tuple-element.28), calls=%async_computation | async-start | bytes 2097152 | tf_op jit(solution)/shard_map/all_to_all | solution.py:269
  14.6 0.0 copy-done
  14.6 0.0 copy-done.4
  14.6 0.0 copy-start.1
  14.6 0.9 copy-done.1
  15.6 0.9 copy-done.5
  16.5 0.8 copy-done.12
  17.3 0.8 copy-done.13
  18.0 0.8 copy-done.14
  18.8 0.8 copy-done.15
  19.5 0.7 shard_map.101
  20.2 0.0 copy-start.2
  20.2 0.7 copy-done.2
  20.9 0.6 copy-done.6
  21.5 0.6 copy-done.8
  22.1 0.6 copy-done.10
  22.7 11.5 %all-to-all-done = bf16[128,32,128]{2,1,0:T(8,128)(2,1)S(1)} async-done(((bf16[128,32,128]{2,1,0:T(8,128)(2,1)}), bf16[128,32,128]{2,1,0:T(8,128)(2,1)S(1)}, u32[]{:S(2)}, u32[]{:S(2)}) %all-to-all-start) | async-done | bytes 1048608 | tf_op jit(solution)/shard_map/all_to_all | solution.py:269
  34.2 0.7 shard_map.102
  34.9 0.0 copy-start.3
  34.9 0.0 copy-start.11
  34.9 0.0 copy-start.16
  35.0 17.3 %all_to_all.20.mixed_ref = bf16[128,16,128]{2,1,0:T(8,128)(2,1)S(1)} all-to-all(bf16[128,16,128]{2,1,0:T(8,128)(2,1)S(1)} %shard_map.102), channel_id=1, replica_groups=mesh['row'=16,'col'=8] {'row','col'}, dimensions={0} | all-to-all | bytes 1048576 | tf_op jit(solution)/shard_map/all_to_all | solution.py:269
  52.2 0.0 copy-done.3
  52.3 0.0 copy-done.11
  52.3 1.7 %shard_map.103 = (bf16[128,32,128]{2,1,0:T(8,128)(2,1)S(1)}, bf16[128,2048]{1,0:T(8,128)(2,1)S(1)}, f32[128,2048]{1,0:T(8,128)S(1)}) custom-call(bf16[128,16,128]{2,1,0:T(8,128)(2,1)S(1)} %all_to_all.20.mixed_ref, f32[16,128]{1,0:T(8,128)S(1)} %copy-done.16, bf16[128,2048]{1,0:T(8,128)(2,1)S(1)} %get-tuple-element.39.res_ref, ...), custom_call_target="tpu_custom_call" | custom-call | tf_op jit(solution)/shard_map/pallas_call | solution.py:215
  54.0 23.3 %all_to_all.21 = bf16[128,32,128]{2,1,0:T(8,128)(2,1)S(1)} all-to-all(bf16[128,32,128]{2,1,0:T(8,128)(2,1)S(1)} %get-tuple-element.43), channel_id=1, replica_groups=mesh['row'=16,'col'=8] {'row','col'}, dimensions={0} | all-to-all | bytes 2097152 | tf_op jit(solution)/shard_map/all_to_all | solution.py:269
  77.3 0.9 shard_map.104
  78.2 16.1 %all_to_all.22.mixed_ref = bf16[128,16,128]{2,1,0:T(8,128)(2,1)S(1)} all-to-all(bf16[128,16,128]{2,1,0:T(8,128)(2,1)S(1)} %shard_map.104), channel_id=1, replica_groups={{77,69,109,101,93,85,79,71,75,67,92,84,45,37,125,117,111,103,107,99,124..., dimensions={0} | all-to-all | bytes 1048576 | tf_op jit(solution)/shard_map/all_to_all | solution.py:269
  94.4 3.0 %shard_map.105 = bf16[32,64,128]{2,1,0:T(8,128)(2,1)} custom-call(bf16[128,16,128]{2,1,0:T(8,128)(2,1)S(1)} %all_to_all.22.mixed_ref, bf16[128,2048]{1,0:T(8,128)(2,1)S(1)} %get-tuple-element.44.res_ref, f32[128,2048]{1,0:T(8,128)S(1)} %get-tuple-element.45.gate_ref, bf16[128,128]{1,0:T(8,128)(2,1)S(1)} %copy-done.9, ...), custom_call_target="tpu_custom_call" | custom-call | tf_op jit(solution)/shard_map/pallas_call | solution.py:215
  (13 shorter events, 0.0 us)
Async XLA Ops:
  3.1 11.5 %copy-start = (bf16[32,64,128]{2,1,0:T(8,128)(2,1)S(1)}, bf16[32,64,128]{2,1,0:T(8,128)(2,1)}, u32[]{:S(2)}) copy-start(bf16[32,64,128]{2,1,0:T(8,128)(2,1)} %pair_ref) | copy-start | bytes 1572868
  3.1 11.5 %copy-start.4 = (bf16[128,512]{1,0:T(8,128)(2,1)S(1)}, bf16[128,512]{1,0:T(8,128)(2,1)}, u32[]{:S(2)}) copy-start(bf16[128,512]{1,0:T(8,128)(2,1)} %in_w_ref.1) | copy-start | bytes 393220
  3.1 31.1 %all-to-all-start = ((bf16[128,32,128]{2,1,0:T(8,128)(2,1)}), bf16[128,32,128]{2,1,0:T(8,128)(2,1)S(1)}, u32[]{:S(2)}, u32[]{:S(2)}) async-start(bf16[128,32,128]{2,1,0:T(8,128)(2,1)} %get-tuple-element.28), calls=%async_computation | async-start | bytes 2097152 | tf_op jit(solution)/shard_map/all_to_all | solution.py:269
  14.6 1.0 copy-start.1
  15.6 0.9 copy-start.5
  16.5 0.8 copy-start.12
  17.3 0.8 copy-start.13
  18.0 0.8 copy-start.14
  18.8 0.8 copy-start.15
  20.2 0.7 copy-start.2
  20.9 0.7 copy-start.6
  21.5 0.6 copy-start.8
  22.1 0.6 copy-start.10
  34.9 17.3 %copy-start.3 = (bf16[640,128]{1,0:T(8,128)(2,1)S(1)}, bf16[640,128]{1,0:T(8,128)(2,1)}, u32[]{:S(2)}) copy-start(bf16[640,128]{1,0:T(8,128)(2,1)} %copy-done.2) | copy-start | bytes 491524
  34.9 17.3 %copy-start.11 = (bf16[128,128]{1,0:T(8,128)(2,1)S(1)}, bf16[128,128]{1,0:T(8,128)(2,1)}, u32[]{:S(2)}) copy-start(bf16[128,128]{1,0:T(8,128)(2,1)} %copy-done.10) | copy-start | bytes 98308
  34.9 17.3 %copy-start.16 = (f32[16,128]{1,0:T(8,128)S(1)}, f32[16,128]{1,0:T(8,128)}, u32[]{:S(2)}) copy-start(f32[16,128]{1,0:T(8,128)} %get-tuple-element.38.mask_ref) | copy-start | bytes 24580
  78.2 16.2 %copy-start.7 = (bf16[128,512]{1,0:T(8,128)(2,1)S(1)}, bf16[128,512]{1,0:T(8,128)(2,1)}, u32[]{:S(2)}) copy-start(bf16[128,512]{1,0:T(8,128)(2,1)} %copy-done.6) | copy-start | bytes 393220
  78.2 16.2 %copy-start.9 = (bf16[128,128]{1,0:T(8,128)(2,1)S(1)}, bf16[128,128]{1,0:T(8,128)(2,1)}, u32[]{:S(2)}) copy-start(bf16[128,128]{1,0:T(8,128)(2,1)} %copy-done.8) | copy-start | bytes 98308

commit v7 on v5

--- a/solution.py
+++ b/solution.py
@@ -130,7 +130,9 @@
             whole[:, 1, :, lanes] = bottom.reshape(16, HALF, LANES)
     lhs = left[...].reshape(512, 512)
     rhs = right[...].reshape(512, 512)
-    dims = (((0,), (0,)), ((), ())) if incoming else (((1,), (1,)), ((), ()))
+    if incoming:
+        lhs = lhs.astype(F32).T.astype(BF16)
+    dims = (((1,), (0 if incoming else 1,)), ((), ()))
     mixed = lax.dot_general(lhs, rhs, dims, preferred_element_type=F32).astype(BF16)
     mixed = mixed.reshape(16, 2, HALF, 512)
     for pair in range(4):

time: 98.1 us -> 98 us (level)
  no operation moved by 1% of the time
where the time goes in v7:
time: 98 us; the launch traced here: 97.4 us
  blocking collectives  56.7 us (58%)
  starting transfers between devices  11.5 us (12%)
  waiting for transfers between devices  11.5 us (12%)
  Pallas kernels  10.2 us (10%)
  local copies, waits for them, and re-layouts  7.42 us (8%)
    all_to_all x3, blocking collectives, exchange(): lax.all_to_all(x, ('row', 'col'), 0, 0, axis_index_groups=groups, tiled=T...  56.7 us
    all_to_all x1, starting transfers between devices, exchange(): lax.all_to_all(x, ('row', 'col'), 0, 0, axis_index_groups=groups, tiled=T...  11.5 us
    all_to_all x1, waiting for transfers between devices, exchange(): lax.all_to_all(x, ('row', 'col'), 0, 0, axis_index_groups=groups, tiled=T...  11.5 us
    unnamed x34, local copies, waits for them, and re-layouts  7.42 us
    pallas_call x5, Pallas kernels, local(): pl.pallas_call(kernel, out_shape=out, in_specs=[VMEM] * len(args), out_sp...  7.1 us
    pallas_call x1, Pallas kernels, first(): pl.pallas_call(first_kernel, out_shape=(PIECES, MASK), in_specs=[ANY] * 3...  3.07 us
  transfers between devices with their start and end apart: 1, of which 1 were waited for; matrix products, arithmetic and copies ran while one was open for 0% of the time, Pallas kernels for 1%

profile of v7, /device:TPU:1, one launch (start us, length us, event | category | flops | bytes accessed | tf_op | source)
XLA Modules:
  0.0 97.4 jit_solution(12739007315573839733)
XLA Ops:
  0.0 3.1 %shard_map.100 = (bf16[128,32,128]{2,1,0:T(8,128)(2,1)}, f32[16,128]{1,0:T(8,128)}) custom-call(bf16[32,64,128]{2,1,0:T(8,128)(2,1)} %pair_ref, bf16[128,512]{1,0:T(8,128)(2,1)} %w_in_hbm.1, s32[4,128]{1,0:T(4,128)} %bitcast.5), custom_call_target="tpu_custom_call" | custom-call | tf_op jit(solution)/shard_map/pallas_call | solution.py:223
  3.1 0.0 copy-start
  3.1 0.0 copy-start.4
  3.1 11.5 %all-to-all-start = ((bf16[128,32,128]{2,1,0:T(8,128)(2,1)}), bf16[128,32,128]{2,1,0:T(8,128)(2,1)S(1)}, u32[]{:S(2)}, u32[]{:S(2)}) async-start(bf16[128,32,128]{2,1,0:T(8,128)(2,1)} %get-tuple-element.28), calls=%async_computation | async-start | bytes 2097152 | tf_op jit(solution)/shard_map/all_to_all | solution.py:265
  14.6 0.0 copy-done
  14.6 0.0 copy-done.4
  14.6 0.0 copy-start.1
  14.6 0.9 copy-done.1
  15.6 0.9 copy-done.5
  16.5 0.8 copy-done.12
  17.3 0.8 copy-done.13
  18.0 0.8 copy-done.14
  18.8 0.8 copy-done.15
  19.5 0.7 shard_map.101
  20.2 0.0 copy-start.2
  20.2 0.7 copy-done.2
  20.9 0.6 copy-done.6
  21.5 0.6 copy-done.8
  22.1 0.6 copy-done.10
  22.7 11.5 %all-to-all-done = bf16[128,32,128]{2,1,0:T(8,128)(2,1)S(1)} async-done(((bf16[128,32,128]{2,1,0:T(8,128)(2,1)}), bf16[128,32,128]{2,1,0:T(8,128)(2,1)S(1)}, u32[]{:S(2)}, u32[]{:S(2)}) %all-to-all-start) | async-done | bytes 1048608 | tf_op jit(solution)/shard_map/all_to_all | solution.py:265
  34.2 0.7 shard_map.102
  34.9 0.0 copy-start.3
  34.9 0.0 copy-start.11
  34.9 0.0 copy-start.16
  35.0 17.3 %all_to_all.20.mixed_ref = bf16[128,16,128]{2,1,0:T(8,128)(2,1)S(1)} all-to-all(bf16[128,16,128]{2,1,0:T(8,128)(2,1)S(1)} %shard_map.102), channel_id=1, replica_groups=mesh['row'=16,'col'=8] {'row','col'}, dimensions={0} | all-to-all | bytes 1048576 | tf_op jit(solution)/shard_map/all_to_all | solution.py:265
  52.2 0.0 copy-done.3
  52.3 0.0 copy-done.11
  52.3 1.7 %shard_map.103 = (bf16[128,32,128]{2,1,0:T(8,128)(2,1)S(1)}, bf16[128,2048]{1,0:T(8,128)(2,1)S(1)}, f32[128,2048]{1,0:T(8,128)S(1)}) custom-call(bf16[128,16,128]{2,1,0:T(8,128)(2,1)S(1)} %all_to_all.20.mixed_ref, f32[16,128]{1,0:T(8,128)S(1)} %copy-done.16, bf16[128,2048]{1,0:T(8,128)(2,1)S(1)} %get-tuple-element.39.res_ref, ...), custom_call_target="tpu_custom_call" | custom-call | tf_op jit(solution)/shard_map/pallas_call | solution.py:211
  54.0 23.3 %all_to_all.21 = bf16[128,32,128]{2,1,0:T(8,128)(2,1)S(1)} all-to-all(bf16[128,32,128]{2,1,0:T(8,128)(2,1)S(1)} %get-tuple-element.43), channel_id=1, replica_groups=mesh['row'=16,'col'=8] {'row','col'}, dimensions={0} | all-to-all | bytes 2097152 | tf_op jit(solution)/shard_map/all_to_all | solution.py:265
  77.3 0.9 shard_map.104
  78.3 16.1 %all_to_all.22.mixed_ref = bf16[128,16,128]{2,1,0:T(8,128)(2,1)S(1)} all-to-all(bf16[128,16,128]{2,1,0:T(8,128)(2,1)S(1)} %shard_map.104), channel_id=1, replica_groups={{77,69,109,101,93,85,79,71,75,67,92,84,45,37,125,117,111,103,107,99,124..., dimensions={0} | all-to-all | bytes 1048576 | tf_op jit(solution)/shard_map/all_to_all | solution.py:265
  94.4 3.0 %shard_map.105 = bf16[32,64,128]{2,1,0:T(8,128)(2,1)} custom-call(bf16[128,16,128]{2,1,0:T(8,128)(2,1)S(1)} %all_to_all.22.mixed_ref, bf16[128,2048]{1,0:T(8,128)(2,1)S(1)} %get-tuple-element.44.res_ref, f32[128,2048]{1,0:T(8,128)S(1)} %get-tuple-element.45.gate_ref, bf16[128,128]{1,0:T(8,128)(2,1)S(1)} %copy-done.9, ...), custom_call_target="tpu_custom_call" | custom-call | tf_op jit(solution)/shard_map/pallas_call | solution.py:211
  (13 shorter events, 0.0 us)
Async XLA Ops:
  3.1 11.5 %copy-start = (bf16[32,64,128]{2,1,0:T(8,128)(2,1)S(1)}, bf16[32,64,128]{2,1,0:T(8,128)(2,1)}, u32[]{:S(2)}) copy-start(bf16[32,64,128]{2,1,0:T(8,128)(2,1)} %pair_ref) | copy-start | bytes 1572868
  3.1 11.5 %copy-start.4 = (bf16[128,512]{1,0:T(8,128)(2,1)S(1)}, bf16[128,512]{1,0:T(8,128)(2,1)}, u32[]{:S(2)}) copy-start(bf16[128,512]{1,0:T(8,128)(2,1)} %in_w_ref.1) | copy-start | bytes 393220
  3.1 31.1 %all-to-all-start = ((bf16[128,32,128]{2,1,0:T(8,128)(2,1)}), bf16[128,32,128]{2,1,0:T(8,128)(2,1)S(1)}, u32[]{:S(2)}, u32[]{:S(2)}) async-start(bf16[128,32,128]{2,1,0:T(8,128)(2,1)} %get-tuple-element.28), calls=%async_computation | async-start | bytes 2097152 | tf_op jit(solution)/shard_map/all_to_all | solution.py:265
  14.6 1.0 copy-start.1
  15.6 0.9 copy-start.5
  16.5 0.8 copy-start.12
  17.3 0.8 copy-start.13
  18.0 0.8 copy-start.14
  18.8 0.8 copy-start.15
  20.2 0.7 copy-start.2
  20.9 0.7 copy-start.6
  21.5 0.6 copy-start.8
  22.1 0.6 copy-start.10
  34.9 17.3 %copy-start.3 = (bf16[640,128]{1,0:T(8,128)(2,1)S(1)}, bf16[640,128]{1,0:T(8,128)(2,1)}, u32[]{:S(2)}) copy-start(bf16[640,128]{1,0:T(8,128)(2,1)} %copy-done.2) | copy-start | bytes 491524
  34.9 17.3 %copy-start.11 = (bf16[128,128]{1,0:T(8,128)(2,1)S(1)}, bf16[128,128]{1,0:T(8,128)(2,1)}, u32[]{:S(2)}) copy-start(bf16[128,128]{1,0:T(8,128)(2,1)} %copy-done.10) | copy-start | bytes 98308
  34.9 17.3 %copy-start.16 = (f32[16,128]{1,0:T(8,128)S(1)}, f32[16,128]{1,0:T(8,128)}, u32[]{:S(2)}) copy-start(f32[16,128]{1,0:T(8,128)} %get-tuple-element.38.mask_ref) | copy-start | bytes 24580
  78.2 16.2 %copy-start.7 = (bf16[128,512]{1,0:T(8,128)(2,1)S(1)}, bf16[128,512]{1,0:T(8,128)(2,1)}, u32[]{:S(2)}) copy-start(bf16[128,512]{1,0:T(8,128)(2,1)} %copy-done.6) | copy-start | bytes 393220
  78.2 16.2 %copy-start.9 = (bf16[128,128]{1,0:T(8,128)(2,1)S(1)}, bf16[128,128]{1,0:T(8,128)(2,1)}, u32[]{:S(2)}) copy-start(bf16[128,128]{1,0:T(8,128)(2,1)} %copy-done.8) | copy-start | bytes 98308

commit v8 on v7

--- a/solution.py
+++ b/solution.py
@@ -106,7 +106,7 @@
         lanes = slice(s * LANES, (s + 8) * LANES)
         x = load_steps(pair_ref, s, 8)
         res_ref[:, lanes] = x
-        gate_ref[:, lanes] = sigmoid(project(x.astype(F32), w))
+        gate_ref[:, lanes] = sigmoid(project(x.astype(F32), w)).astype(BF16)
     out_t_ref[...] = out_w_ref[...].T
     in_t_ref[:512] = in_w_ref[...].T
     in_t_ref[512:] = next_gate_w_ref[...].T
@@ -163,7 +163,7 @@
     lanes = slice(s0 * LANES, (s0 + count) * LANES)
     scaled = jnp.concatenate([scaled_step(rows, s0 + n) for n in range(count)], axis=1)
     update = jnp.dot(w_out, scaled, preferred_element_type=F32)
-    return (res_ref[:, lanes].astype(F32) + gate_ref[:, lanes] * update).astype(BF16)
+    return (res_ref[:, lanes].astype(F32) + gate_ref[:, lanes].astype(F32) * update).astype(BF16)
 
 
 def middle_kernel(
@@ -175,7 +175,7 @@
     first_ref[...] = x
     p = project(x.astype(F32), w_in_ref[...])
     stage_operands(p, mask_ref, stage)
-    next_gate_ref[...] = sigmoid(p[512:])
+    next_gate_ref[...] = sigmoid(p[512:]).astype(BF16)
     put_pieces(stage, pieces_ref)
 
 
@@ -200,7 +200,7 @@
 PIECES = jax.ShapeDtypeStruct((DEVS, 2 * HALF, LANES), BF16)
 MASK = jax.ShapeDtypeStruct((HALF, LANES), F32)
 MIXED = jax.ShapeDtypeStruct((DEVS, HALF, LANES), BF16)
-GATE = jax.ShapeDtypeStruct((CHANS, SPOTS), F32)
+GATE = jax.ShapeDtypeStruct((CHANS, SPOTS), BF16)
 RES = jax.ShapeDtypeStruct((CHANS, SPOTS), BF16)
 TILE = jax.ShapeDtypeStruct((ROWS, COLS, CHANS), BF16)
 STAGE_T = pltpu.VMEM(((DEVS + 1) * STAGE, LANES), F32)

time: 98 us -> 97.9 us (level)
  local copies, waits for them, and re-layouts: 7.42 us -> 3.86 us
  waiting for transfers between devices: 11.5 us -> 15 us
    unnamed x34 -> x22, local copies, waits for them, and re-layouts: 7.42 us -> 3.86 us
    all_to_all x1, waiting for transfers between devices: 11.5 us -> 15 us  [exchange(): lax.all_to_all(x, ('row', 'col'), 0, 0, axis_index_groups=groups, tiled=T...]
where the time goes in v8:
time: 97.9 us; the launch traced here: 97.4 us
  blocking collectives  56.7 us (58%)
  waiting for transfers between devices  15 us (15%)
  starting transfers between devices  11.5 us (12%)
  Pallas kernels  10.2 us (10%)
  local copies, waits for them, and re-layouts  3.86 us (4%)
    all_to_all x3, blocking collectives, exchange(): lax.all_to_all(x, ('row', 'col'), 0, 0, axis_index_groups=groups, tiled=T...  56.7 us
    all_to_all x1, waiting for transfers between devices, exchange(): lax.all_to_all(x, ('row', 'col'), 0, 0, axis_index_groups=groups, tiled=T...  15 us
    all_to_all x1, starting transfers between devices, exchange(): lax.all_to_all(x, ('row', 'col'), 0, 0, axis_index_groups=groups, tiled=T...  11.5 us
    pallas_call x5, Pallas kernels, local(): pl.pallas_call(kernel, out_shape=out, in_specs=[VMEM] * len(args), out_sp...  7.13 us
    unnamed x22, local copies, waits for them, and re-layouts  3.86 us
    pallas_call x1, Pallas kernels, first(): pl.pallas_call(first_kernel, out_shape=(PIECES, MASK), in_specs=[ANY] * 3...  3.07 us
  transfers between devices with their start and end apart: 1, of which 1 were waited for; matrix products, arithmetic and copies ran while one was open for 0% of the time, Pallas kernels for 1%

profile of v8, /device:TPU:1, one launch (start us, length us, event | category | flops | bytes accessed | tf_op | source)
XLA Modules:
  0.0 97.4 jit_solution(2156809080650094485)
XLA Ops:
  0.0 3.1 %shard_map.100 = (bf16[128,32,128]{2,1,0:T(8,128)(2,1)}, f32[16,128]{1,0:T(8,128)}) custom-call(bf16[32,64,128]{2,1,0:T(8,128)(2,1)} %pair_ref, bf16[128,512]{1,0:T(8,128)(2,1)} %w_in_hbm.1, s32[4,128]{1,0:T(4,128)} %bitcast.5), custom_call_target="tpu_custom_call" | custom-call | tf_op jit(solution)/shard_map/pallas_call | solution.py:223
  3.1 0.0 copy-start
  3.1 0.0 copy-start.1
  3.1 0.0 copy-start.2
  3.1 0.0 copy-start.6
  3.1 11.5 %all-to-all-start = ((bf16[128,32,128]{2,1,0:T(8,128)(2,1)}), bf16[128,32,128]{2,1,0:T(8,128)(2,1)S(1)}, u32[]{:S(2)}, u32[]{:S(2)}) async-start(bf16[128,32,128]{2,1,0:T(8,128)(2,1)} %get-tuple-element.28), calls=%async_computation | async-start | bytes 2097152 | tf_op jit(solution)/shard_map/all_to_all | solution.py:265
  14.6 0.0 copy-done
  14.6 0.0 copy-done.1
  14.7 0.0 copy-done.2
  14.7 0.0 copy-done.6
  14.7 0.0 copy-start.3
  14.7 0.9 copy-done.3
  15.6 0.0 copy-start.7
  15.6 0.8 copy-done.7
  16.3 0.0 copy-start.8
  16.3 0.8 copy-done.8
  17.1 0.8 copy-done.9
  17.9 0.7 shard_map.101
  18.6 0.0 copy-start.4
  18.6 0.6 copy-done.4
  19.2 15.0 %all-to-all-done = bf16[128,32,128]{2,1,0:T(8,128)(2,1)S(1)} async-done(((bf16[128,32,128]{2,1,0:T(8,128)(2,1)}), bf16[128,32,128]{2,1,0:T(8,128)(2,1)S(1)}, u32[]{:S(2)}, u32[]{:S(2)}) %all-to-all-start) | async-done | bytes 1048608 | tf_op jit(solution)/shard_map/all_to_all | solution.py:265
  34.2 0.7 shard_map.102
  34.9 0.0 copy-start.10
  35.0 17.3 %all_to_all.20.mixed_ref = bf16[128,16,128]{2,1,0:T(8,128)(2,1)S(1)} all-to-all(bf16[128,16,128]{2,1,0:T(8,128)(2,1)S(1)} %shard_map.102), channel_id=1, replica_groups=mesh['row'=16,'col'=8] {'row','col'}, dimensions={0} | all-to-all | bytes 1048576 | tf_op jit(solution)/shard_map/all_to_all | solution.py:265
  52.2 0.0 copy-done.10
  52.2 1.8 %shard_map.103 = (bf16[128,32,128]{2,1,0:T(8,128)(2,1)S(1)}, bf16[128,2048]{1,0:T(8,128)(2,1)S(1)}, bf16[128,2048]{1,0:T(8,128)(2,1)S(1)}) custom-call(bf16[128,16,128]{2,1,0:T(8,128)(2,1)S(1)} %all_to_all.20.mixed_ref, f32[16,128]{1,0:T(8,128)S(1)} %copy-done.10, bf16[128,2048]{1,0:T(8,128)(2,1)S(1)} %get-tuple-element.39.res_ref, ...), custom_call_target="tpu_custom_call" | custom-call | tf_op jit(solution)/shard_map/pallas_call | solution.py:211
  54.0 23.3 %all_to_all.21 = bf16[128,32,128]{2,1,0:T(8,128)(2,1)S(1)} all-to-all(bf16[128,32,128]{2,1,0:T(8,128)(2,1)S(1)} %get-tuple-element.43), channel_id=1, replica_groups=mesh['row'=16,'col'=8] {'row','col'}, dimensions={0} | all-to-all | bytes 2097152 | tf_op jit(solution)/shard_map/all_to_all | solution.py:265
  77.3 0.9 shard_map.104
  78.3 0.0 copy-start.5
  78.3 16.1 %all_to_all.22.mixed_ref = bf16[128,16,128]{2,1,0:T(8,128)(2,1)S(1)} all-to-all(bf16[128,16,128]{2,1,0:T(8,128)(2,1)S(1)} %shard_map.104), channel_id=1, replica_groups={{77,69,109,101,93,85,79,71,75,67,92,84,45,37,125,117,111,103,107,99,124..., dimensions={0} | all-to-all | bytes 1048576 | tf_op jit(solution)/shard_map/all_to_all | solution.py:265
  94.4 0.0 copy-done.5
  94.4 3.0 %shard_map.105 = bf16[32,64,128]{2,1,0:T(8,128)(2,1)} custom-call(bf16[128,16,128]{2,1,0:T(8,128)(2,1)S(1)} %all_to_all.22.mixed_ref, bf16[128,2048]{1,0:T(8,128)(2,1)S(1)} %get-tuple-element.44.res_ref, bf16[128,2048]{1,0:T(8,128)(2,1)S(1)} %get-tuple-element.45.gate_ref, bf16[128,128]{1,0:T(8,128)(2,1)S(1)} %get-tuple-element.46.w_out_ref, ...), custom_call_target="tpu_custom_call" | custom-call | tf_op jit(solution)/shard_map/pallas_call | solution.py:211
  (1 shorter events, 0.0 us)
Async XLA Ops:
  3.1 11.6 %copy-start = (bf16[32,64,128]{2,1,0:T(8,128)(2,1)S(1)}, bf16[32,64,128]{2,1,0:T(8,128)(2,1)}, u32[]{:S(2)}) copy-start(bf16[32,64,128]{2,1,0:T(8,128)(2,1)} %pair_ref) | copy-start | bytes 1572868
  3.1 11.6 %copy-start.1 = (bf16[128,1024]{1,0:T(8,128)(2,1)S(1)}, bf16[128,1024]{1,0:T(8,128)(2,1)}, u32[]{:S(2)}) copy-start(bf16[128,1024]{1,0:T(8,128)(2,1)} %up_ref.1) | copy-start | bytes 786436
  3.1 11.6 %copy-start.2 = (bf16[128,512]{1,0:T(8,128)(2,1)S(1)}, bf16[128,512]{1,0:T(8,128)(2,1)}, u32[]{:S(2)}) copy-start(bf16[128,512]{1,0:T(8,128)(2,1)} %in_w_ref.1) | copy-start | bytes 393220
  3.1 11.6 %copy-start.6 = (bf16[128,128]{1,0:T(8,128)(2,1)S(1)}, bf16[128,128]{1,0:T(8,128)(2,1)}, u32[]{:S(2)}) copy-start(bf16[128,128]{1,0:T(8,128)(2,1)} %gate_w_ref.1) | copy-start | bytes 98308
  3.1 31.1 %all-to-all-start = ((bf16[128,32,128]{2,1,0:T(8,128)(2,1)}), bf16[128,32,128]{2,1,0:T(8,128)(2,1)S(1)}, u32[]{:S(2)}, u32[]{:S(2)}) async-start(bf16[128,32,128]{2,1,0:T(8,128)(2,1)} %get-tuple-element.28), calls=%async_computation | async-start | bytes 2097152 | tf_op jit(solution)/shard_map/all_to_all | solution.py:265
  14.7 0.9 copy-start.3
  15.6 0.8 copy-start.7
  16.3 0.8 copy-start.8
  17.1 0.8 copy-start.9
  18.6 0.7 copy-start.4
  34.9 17.3 %copy-start.10 = (f32[16,128]{1,0:T(8,128)S(1)}, f32[16,128]{1,0:T(8,128)}, u32[]{:S(2)}) copy-start(f32[16,128]{1,0:T(8,128)} %get-tuple-element.38.mask_ref) | copy-start | bytes 24580
  78.3 16.2 %copy-start.5 = (bf16[128,512]{1,0:T(8,128)(2,1)S(1)}, bf16[128,512]{1,0:T(8,128)(2,1)}, u32[]{:S(2)}) copy-start(bf16[128,512]{1,0:T(8,128)(2,1)} %copy-done.4) | copy-start | bytes 393220
